TPU v7x, 32 devices: a whole 2x2x4 slice. The times are simulated.
32 devices in a mesh: section: 2 (over x), ctx: 8 (over z, core), wshard: 2 (over y).
Axes of the slice: x: 2, y: 2, z: 4, core: 2. Of those that a mesh axis runs over, the one named last changes fastest.
Arguments:
- tokens: bfloat16 [2, 2, 1024, 768], P(None, 'wshard', 'ctx'), may hold values from -6 to 6
- block_order: int32 [2, 2, 8], P(None, 'wshard'), may hold values from 0 to 7, each once within a row
- cotangent: bfloat16 [2, 2, 1024, 768], P(None, 'wshard', 'ctx'), may hold values from -6 to 6
- attn_gain: bfloat16 [2, 768], P('section', ('ctx', 'wshard')), may hold values from 0.099609375 to 1.8984375
- qkv_weight: bfloat16 [2, 768, 2304], P('section', ('ctx', 'wshard')), may hold values from -0.21875 to 0.21875
- out_weight: bfloat16 [2, 768, 768], P('section', ('ctx', 'wshard')), may hold values from -5 to 5
- mlp_gain: bfloat16 [2, 768], P('section', ('ctx', 'wshard')), may hold values from 0.099609375 to 1.8984375
- in_weight: bfloat16 [2, 768, 2304], P('section', ('ctx', 'wshard')), may hold values from -0.21875 to 0.21875
- down_weight: bfloat16 [2, 1152, 768], P('section', ('ctx', 'wshard')), may hold values from -0.1875 to 0.1875
Outputs:
- activations: bfloat16 [2, 2, 2, 1024, 768], P('section', None, 'wshard', 'ctx')
- input_grads: float32 [2, 2, 2, 1024, 768], P('section', None, 'wshard', 'ctx')
- attn_gain_grad: float32 [2, 768], P('section', ('ctx', 'wshard'))
- qkv_grad: float32 [2, 768, 2304], P('section', ('ctx', 'wshard'))
- out_grad: float32 [2, 768, 768], P('section', ('ctx', 'wshard'))
- mlp_gain_grad: float32 [2, 768], P('section', ('ctx', 'wshard'))
- in_grad: float32 [2, 768, 2304], P('section', ('ctx', 'wshard'))
- down_grad: float32 [2, 1152, 768], P('section', ('ctx', 'wshard'))
Inputs may be any that keep to these rules, and one draw needn't show every extreme that they name: Each block_order[m, w, :] is a permutation of the cycle devices: every block of 128 positions of a sequence sits on exactly one device.
All inputs are finite; a program needn't handle non-finite values.
Results may differ from a plain program's by a relative error of at most 0.03.
Values may be sent and summed in bfloat16 or wider, within the bound.
A program may use at most 256 MiB of HBM per device.

v0:
```python
import jax
import jax.numpy as jnp
from jax import lax
from jax.sharding import PartitionSpec as P

D = 768
HEADS = 12
HEAD_DIM = 64
FF = 1152


epsilon = 1e-05
rope_base = 160000.0


def shifted(x, axis, by):
    peers = lax.axis_size(axis)
    pairs = [(i, i + by) for i in range(peers) if 0 <= i + by < peers]
    return lax.ppermute(x, axis, pairs)


def normalize(values):
    row_mean = jnp.mean(values, axis=-1, keepdims=True)
    centered = values - row_mean
    variance = jnp.mean(centered * centered, axis=-1, keepdims=True)
    inverse = lax.rsqrt(variance + epsilon)
    return (centered * inverse, inverse)


def norm_back(grad_hat, normed, inverse):
    first_mean = jnp.mean(grad_hat, axis=-1, keepdims=True)
    second_mean = jnp.mean(grad_hat * normed, axis=-1, keepdims=True)
    return (grad_hat - first_mean - normed * second_mean) * inverse


def split_heads(values):
    return values.reshape(values.shape[0], HEADS, HEAD_DIM)


def join_heads(values):
    return values.reshape(values.shape[0], HEADS * HEAD_DIM)


def rotate_half(values):
    half_width = values.shape[-1] // 2
    return jnp.concatenate([-values[..., half_width:], values[..., :half_width]], axis=-1)


def rotate_back(values):
    half_width = values.shape[-1] // 2
    return jnp.concatenate([values[..., half_width:], -values[..., :half_width]], axis=-1)


def rotary(block_id, tok_rows):
    positions = (block_id * tok_rows + jnp.arange(tok_rows, dtype=jnp.int32)).astype(jnp.float32)
    inverse = 1.0 / rope_base ** (jnp.arange(0, HEAD_DIM, 2, dtype=jnp.float32) / HEAD_DIM)
    angles = positions[:, None] * inverse[None, :]
    cosine = jnp.concatenate([jnp.cos(angles), jnp.cos(angles)], axis=-1)[:, None, :]
    sine = jnp.concatenate([jnp.sin(angles), jnp.sin(angles)], axis=-1)[:, None, :]
    return (cosine, sine)


def absorb(state_now, arrived, query_heads):
    largest, running_sum, weighted = state_now
    key_rows, value_rows = arrived
    scores = jnp.einsum(
        "qhe,khe->hqk", query_heads, split_heads(key_rows), preferred_element_type=jnp.float32
    ) * HEAD_DIM ** (-0.5)
    new_max = jnp.maximum(largest, jnp.max(scores, axis=-1))
    shrink = jnp.exp(largest - new_max)
    exponents = jnp.exp(scores - new_max[:, :, None])
    running_sum = jnp.sum(exponents, axis=-1)
    weighted = weighted * shrink.T[:, :, None] + jnp.einsum(
        "hqk,khe->qhe",
        exponents.astype(jnp.bfloat16),
        split_heads(value_rows),
        preferred_element_type=jnp.float32,
    )
    return (new_max, running_sum, weighted)


def score_grads(query_heads, grad_heads, log_sums, deltas, key_heads, value_heads):
    scores = jnp.einsum(
        "qhe,khe->hqk", query_heads, key_heads, preferred_element_type=jnp.float32
    ) * HEAD_DIM ** (-0.5)
    weights = jnp.exp(scores - log_sums.T[:, :, None])
    upstream = jnp.einsum(
        "qhe,khe->hqk", grad_heads, value_heads, preferred_element_type=jnp.float32
    )
    grad_scores = (weights * (upstream - deltas.T[:, :, None])).astype(jnp.bfloat16)
    return (weights.astype(jnp.bfloat16), grad_scores)


def key_value_terms(query_heads, grad_heads, log_sums, deltas, key_heads, value_heads):
    weights_low, grad_scores = score_grads(
        query_heads, grad_heads, log_sums, deltas, key_heads, value_heads
    )
    key_part = jnp.einsum(
        "hqk,qhe->khe", grad_scores, query_heads, preferred_element_type=jnp.float32
    ) * HEAD_DIM ** (-0.5)
    value_part = jnp.einsum(
        "hqk,qhe->khe", weights_low, grad_heads, preferred_element_type=jnp.float32
    )
    return (key_part, value_part)


def forward_layer(layer_in, cosine, sine, params):
    gain_one, w_qkv, w_out, gain_two, w_in, w_down = params
    tok_rows = layer_in.shape[0]
    normed_one, _ = normalize(layer_in)
    mixed = jnp.dot(
        (normed_one * gain_one.astype(jnp.float32)).astype(jnp.bfloat16),
        w_qkv,
        preferred_element_type=jnp.float32,
    )
    query_raw = split_heads(mixed[:, :D])
    key_raw = split_heads(mixed[:, D : 2 * D])
    query_heads = (query_raw * cosine + rotate_half(query_raw) * sine).astype(jnp.bfloat16)
    key_rows = join_heads(key_raw * cosine + rotate_half(key_raw) * sine).astype(jnp.bfloat16)
    value_rows = mixed[:, 2 * D :].astype(jnp.bfloat16)
    start_state = (
        jnp.full((HEADS, tok_rows), -1e30, jnp.float32),
        jnp.zeros((HEADS, tok_rows), jnp.float32),
        jnp.zeros((tok_rows, HEADS, HEAD_DIM), jnp.float32),
    )
    key_rows, value_rows = (
        lax.all_gather(key_rows, "ctx", axis=0, tiled=True),
        lax.all_gather(value_rows, "ctx", axis=0, tiled=True),
    )
    final_state = absorb(start_state, (key_rows, value_rows), query_heads)
    largest, running_sum, weighted = final_state
    attended = join_heads(weighted / running_sum.T[:, :, None])
    log_sums = (largest + jnp.log(running_sum)).T
    hidden = layer_in + jnp.dot(
        attended.astype(jnp.bfloat16), w_out, preferred_element_type=jnp.float32
    )
    normed_two, _ = normalize(hidden)
    gate_up = jnp.dot(
        (normed_two * gain_two.astype(jnp.float32)).astype(jnp.bfloat16),
        w_in,
        preferred_element_type=jnp.float32,
    )
    product = (jax.nn.gelu(gate_up[:, :FF], approximate=False) * gate_up[:, FF:]).astype(
        jnp.bfloat16
    )
    layer_out = hidden + jnp.dot(product, w_down, preferred_element_type=jnp.float32)
    return (
        layer_out,
        (layer_in, hidden, gate_up, query_heads, key_rows, value_rows, attended, log_sums),
    )


def backward_layer(upstream, cosine, sine, params, saved, cycle_place):
    gain_one, w_qkv, w_out, gain_two, w_in, w_down = params
    layer_in, hidden, gate_up, query_heads, key_rows, value_rows, attended, log_sums = saved
    scale_factor = HEAD_DIM ** (-0.5)
    tok_rows = upstream.shape[0]
    grad_branch = upstream.astype(jnp.bfloat16)
    gate_part = gate_up[:, :FF]
    up_part = gate_up[:, FF:]
    activated, gelu_pull = jax.vjp(
        lambda gate_in: jax.nn.gelu(gate_in, approximate=False), gate_part
    )
    product = (activated * up_part).astype(jnp.bfloat16)
    grad_down = jnp.einsum("tf,td->fd", product, grad_branch, preferred_element_type=jnp.float32)
    grad_product = jnp.einsum("td,fd->tf", grad_branch, w_down, preferred_element_type=jnp.float32)
    grad_gate = gelu_pull(grad_product * up_part)[0]
    grad_gate_up = jnp.concatenate([grad_gate, grad_product * activated], axis=-1).astype(
        jnp.bfloat16
    )
    normed_two, inverse_two = normalize(hidden)
    gain_two_full = gain_two.astype(jnp.float32)
    grad_in = jnp.einsum(
        "td,tf->df",
        (normed_two * gain_two_full).astype(jnp.bfloat16),
        grad_gate_up,
        preferred_element_type=jnp.float32,
    )
    grad_normed_two = jnp.einsum(
        "tf,df->td", grad_gate_up, w_in, preferred_element_type=jnp.float32
    )
    grad_gain_two = jnp.sum(grad_normed_two * normed_two, axis=0)
    grad_hidden = upstream + norm_back(grad_normed_two * gain_two_full, normed_two, inverse_two)
    grad_attn_out = grad_hidden.astype(jnp.bfloat16)
    grad_out = jnp.einsum(
        "td,te->de",
        attended.astype(jnp.bfloat16),
        grad_attn_out,
        preferred_element_type=jnp.float32,
    )
    grad_attended = split_heads(
        jnp.einsum("te,de->td", grad_attn_out, w_out, preferred_element_type=jnp.float32).astype(
            jnp.bfloat16
        )
    )
    deltas = jnp.sum(grad_attended.astype(jnp.float32) * split_heads(attended), axis=-1)
    all_logs, all_deltas = (
        lax.all_gather(log_sums, "ctx", axis=0, tiled=True),
        lax.all_gather(deltas, "ctx", axis=0, tiled=True),
    )
    empty_heads = jnp.zeros((tok_rows, HEADS, HEAD_DIM), jnp.float32)
    key_heads = split_heads(key_rows)
    value_heads = split_heads(value_rows)
    _, grad_scores = score_grads(
        query_heads, grad_attended, log_sums, deltas, key_heads, value_heads
    )
    grad_query = (
        jnp.einsum("hqk,khe->qhe", grad_scores, key_heads, preferred_element_type=jnp.float32)
        * scale_factor
    )
    own_start = cycle_place * tok_rows
    own_keys = split_heads(lax.dynamic_slice_in_dim(key_rows, own_start, tok_rows, 0))
    own_values = split_heads(lax.dynamic_slice_in_dim(value_rows, own_start, tok_rows, 0))
    queries_all, grads_all = (
        lax.all_gather(join_heads(query_heads), "ctx", axis=0, tiled=True),
        lax.all_gather(join_heads(grad_attended), "ctx", axis=0, tiled=True),
    )
    total_rows = queries_all.shape[0]
    block_rows = min(512, total_rows)
    block_count = total_rows // block_rows

    def query_block(running, pieces):
        block_queries, block_grads, block_logs, block_deltas = pieces
        key_part, value_part = key_value_terms(
            split_heads(block_queries),
            split_heads(block_grads),
            block_logs,
            block_deltas,
            own_keys,
            own_values,
        )
        return ((running[0] + key_part, running[1] + value_part), None)

    stacked = (
        queries_all.reshape(block_count, block_rows, D),
        grads_all.reshape(block_count, block_rows, D),
        all_logs.reshape(block_count, block_rows, HEADS),
        all_deltas.reshape(block_count, block_rows, HEADS),
    )
    (grad_key, grad_value_heads), _ = lax.scan(query_block, (empty_heads, empty_heads), stacked)
    grad_value = join_heads(grad_value_heads)
    query_grad_raw = grad_query * cosine + rotate_back(grad_query * sine)
    key_grad_raw = grad_key * cosine + rotate_back(grad_key * sine)
    grad_mixed = jnp.concatenate(
        [join_heads(query_grad_raw), join_heads(key_grad_raw), grad_value], axis=-1
    ).astype(jnp.bfloat16)
    normed_one, inverse_one = normalize(layer_in)
    gain_one_full = gain_one.astype(jnp.float32)
    grad_qkv = jnp.einsum(
        "td,tf->df",
        (normed_one * gain_one_full).astype(jnp.bfloat16),
        grad_mixed,
        preferred_element_type=jnp.float32,
    )
    grad_normed_one = jnp.einsum("tf,df->td", grad_mixed, w_qkv, preferred_element_type=jnp.float32)
    grad_gain_one = jnp.sum(grad_normed_one * normed_one, axis=0)
    grad_layer_in = grad_hidden + norm_back(
        grad_normed_one * gain_one_full, normed_one, inverse_one
    )
    return (grad_layer_in, (grad_gain_one, grad_qkv, grad_out, grad_gain_two, grad_in, grad_down))


def keep_slot(buffer, batch_slot, value, is_valid):
    previous = lax.dynamic_index_in_dim(buffer, batch_slot, 0, keepdims=False)
    return lax.dynamic_update_index_in_dim(
        buffer, jnp.where(is_valid, value, previous), batch_slot, 0
    )


def body(
    tokens,
    block_order,
    cotangent,
    attn_gain,
    qkv_weight,
    out_weight,
    mlp_gain,
    in_weight,
    down_weight,
):
    gathered = (
        lax.all_gather(attn_gain, ("ctx", "wshard"), axis=1, tiled=True),
        lax.all_gather(qkv_weight, ("ctx", "wshard"), axis=1, tiled=True),
        lax.all_gather(out_weight, ("ctx", "wshard"), axis=1, tiled=True),
        lax.all_gather(mlp_gain, ("ctx", "wshard"), axis=1, tiled=True),
        lax.all_gather(in_weight, ("ctx", "wshard"), axis=1, tiled=True),
        lax.all_gather(down_weight, ("ctx", "wshard"), axis=1, tiled=True),
    )
    params = tuple((whole[0] for whole in gathered))
    section_id = lax.axis_index("section")
    section_count = lax.axis_size("section")
    cycle_place = lax.axis_index("ctx")
    micro_count = tokens.shape[0]
    tok_rows = tokens.shape[2]
    tick_count = micro_count + section_count - 1
    received = jnp.zeros((tok_rows, D), jnp.bfloat16)
    section_outs = jnp.zeros((micro_count, tok_rows, D), jnp.bfloat16)
    saved_all = None
    for tick in range(tick_count):
        batch_index = tick - section_id
        is_valid = (batch_index >= 0) & (batch_index < micro_count)
        batch_slot = jnp.clip(batch_index, 0, micro_count - 1)
        own_rows = tokens[batch_slot, 0]
        layer_in = jnp.where(section_id == 0, own_rows, received).astype(jnp.float32)
        cosine, sine = rotary(block_order[batch_slot, 0, cycle_place], tok_rows)
        layer_out, saved = forward_layer(layer_in, cosine, sine, params)
        if saved_all is None:
            saved_all = tuple(
                (jnp.zeros((micro_count,) + item.shape, item.dtype) for item in saved)
            )
        saved_all = tuple(
            (
                keep_slot(buffer, batch_slot, item, is_valid)
                for buffer, item in zip(saved_all, saved)
            )
        )
        outgoing = layer_out.astype(jnp.bfloat16)
        section_outs = keep_slot(section_outs, batch_slot, outgoing, is_valid)
        received = shifted(outgoing, "section", 1)
    grad_received = jnp.zeros((tok_rows, D), jnp.bfloat16)
    input_grads = jnp.zeros((micro_count, tok_rows, D), jnp.float32)
    summed = None
    for tick in range(tick_count):
        batch_index = tick - (section_count - 1 - section_id)
        is_valid = (batch_index >= 0) & (batch_index < micro_count)
        batch_slot = jnp.clip(batch_index, 0, micro_count - 1)
        upstream = jnp.where(
            section_id == section_count - 1, cotangent[batch_slot, 0], grad_received
        ).astype(jnp.float32)
        cosine, sine = rotary(block_order[batch_slot, 0, cycle_place], tok_rows)
        saved = tuple(
            (
                lax.dynamic_index_in_dim(buffer, batch_slot, 0, keepdims=False)
                for buffer in saved_all
            )
        )
        grad_layer_in, raw_grads = backward_layer(
            upstream, cosine, sine, params, saved, cycle_place
        )
        weight_grads = tuple(
            (jnp.where(is_valid, grad_term, jnp.zeros_like(grad_term)) for grad_term in raw_grads)
        )
        outgoing = grad_layer_in.astype(jnp.bfloat16)
        kept_grad = jnp.where(section_id == 0, grad_layer_in, outgoing.astype(jnp.float32))
        input_grads = keep_slot(input_grads, batch_slot, kept_grad, is_valid)
        summed = (
            weight_grads
            if summed is None
            else tuple((left + right for left, right in zip(summed, weight_grads)))
        )
        grad_received = shifted(outgoing, "section", -1)
    raised = [grad_term[None] for grad_term in summed]
    summed = (
        lax.psum_scatter(raised[0], ("ctx", "wshard"), scatter_dimension=1, tiled=True),
        lax.psum_scatter(raised[1], ("ctx", "wshard"), scatter_dimension=1, tiled=True),
        lax.psum_scatter(raised[2], ("ctx", "wshard"), scatter_dimension=1, tiled=True),
        lax.psum_scatter(raised[3], ("ctx", "wshard"), scatter_dimension=1, tiled=True),
        lax.psum_scatter(raised[4], ("ctx", "wshard"), scatter_dimension=1, tiled=True),
        lax.psum_scatter(raised[5], ("ctx", "wshard"), scatter_dimension=1, tiled=True),
    )
    return (
        section_outs[None, :, None],
        input_grads[None, :, None],
        summed[0],
        summed[1],
        summed[2],
        summed[3],
        summed[4],
        summed[5],
    )


def solution(mesh):
    in_specs = (
        P(None, "wshard", "ctx", None),
        P(None, "wshard", None),
        P(None, "wshard", "ctx", None),
        P("section", ("ctx", "wshard")),
        P("section", ("ctx", "wshard"), None),
        P("section", ("ctx", "wshard"), None),
        P("section", ("ctx", "wshard")),
        P("section", ("ctx", "wshard"), None),
        P("section", ("ctx", "wshard"), None),
    )
    out_specs = (
        P("section", None, "wshard", "ctx", None),
        P("section", None, "wshard", "ctx", None),
        P("section", ("ctx", "wshard")),
        P("section", ("ctx", "wshard"), None),
        P("section", ("ctx", "wshard"), None),
        P("section", ("ctx", "wshard")),
        P("section", ("ctx", "wshard"), None),
        P("section", ("ctx", "wshard"), None),
    )
    return jax.shard_map(body, mesh=mesh, in_specs=in_specs, out_specs=out_specs, check_vma=False)
```

profile of v0, /device:TPU:0, one launch (start us, length us, event | category | flops | bytes accessed | tf_op | source)
XLA Modules:
  0.0 1220.5 jit_solution(7308023679856398554)
XLA Ops:
  11.6 35.4 %all-reduce.2 = (bf16[768]{0:T(1024)(128)(2,1)S(1)}, bf16[768]{0:T(1024)(128)(2,1)S(1)}) all-reduce(bf16[768]{0:T(1024)(128)(2,1)S(1)} %dynamic-update-slice, bf16[768]{0:T(1024)(128)(2,1)S(1)} %dynamic-update-slice.1), channel_id=1, replica_groups=mesh['section'=2,'ctx'=8,'wshard'=2] {'ctx','wshard'}, use_global_device_ids=true, to_apply=%add | all-reduce | flops 1536 | bytes 6144
  69.7 18.5 %all-gather.22.cloned.1.call-done = bf16[1024,768]{1,0:T(8,128)(2,1)} async-done(((bf16[128,768]{1,0:T(8,128)(2,1)}), bf16[1024,768]{1,0:T(8,128)(2,1)}) %all-gather.22.cloned.1.call-update) | async-done | bytes 1572880 | tf_op jit(solution)/shard_map/all_gather | solution.py:127
  89.9 25.1 %all-gather.24.cloned.1.call-done = bf16[1024,768]{1,0:T(8,128)(2,1)} async-done(((bf16[128,768]{1,0:T(8,128)(2,1)}), bf16[1024,768]{1,0:T(8,128)(2,1)}) %all-gather.24.cloned.1.call-update) | async-done | bytes 1572880 | tf_op jit(solution)/shard_map/all_gather | solution.py:128
  122.4 32.7 %all-gather.26.cloned.1.call-done = bf16[1,768,768]{2,1,0:T(8,128)(2,1)} async-done(((bf16[1,48,768]{2,1,0:T(8,128)(2,1)}), bf16[1,768,768]{2,1,0:T(8,128)(2,1)}) %all-gather.26.cloned.1.call-update) | async-done | bytes 1179664 | tf_op jit(solution)/shard_map/all_gather | solution.py:284
  157.7 45.8 %all-gather.28.cloned.1.call-done = bf16[1,768,2304]{2,1,0:T(8,128)(2,1)} async-done(((bf16[1,48,2304]{2,1,0:T(8,128)(2,1)}), bf16[1,768,2304]{2,1,0:T(8,128)(2,1)}) %all-gather.28.cloned.1.call-update) | async-done | bytes 3538960 | tf_op jit(solution)/shard_map/all_gather | solution.py:286
  209.2 35.8 %all-gather.30.cloned.1.call-done = bf16[1,1152,768]{2,1,0:T(8,128)(2,1)} async-done(((bf16[1,72,768]{2,1,0:T(8,128)(2,1)}), bf16[1,1152,768]{2,1,0:T(8,128)(2,1)}) %all-gather.30.cloned.1.call-update) | async-done | bytes 1769488 | tf_op jit(solution)/shard_map/all_gather | solution.py:287
  274.1 15.4 %all-gather.32.cloned.1.call-done = bf16[1024,768]{1,0:T(8,128)(2,1)} async-done(((bf16[128,768]{1,0:T(8,128)(2,1)}), bf16[1024,768]{1,0:T(8,128)(2,1)}) %all-gather.32.cloned.1.call-update) | async-done | bytes 1572880 | tf_op jit(solution)/shard_map/all_gather | solution.py:127
  298.7 17.1 %all-gather.34.cloned.1.call-done = bf16[1024,768]{1,0:T(8,128)(2,1)} async-done(((bf16[128,768]{1,0:T(8,128)(2,1)}), bf16[1024,768]{1,0:T(8,128)(2,1)}) %all-gather.34.cloned.1.call-update) | async-done | bytes 1572880 | tf_op jit(solution)/shard_map/all_gather | solution.py:128
  358.1 15.6 %all-gather.36.cloned.1.call-done = bf16[1024,768]{1,0:T(8,128)(2,1)} async-done(((bf16[128,768]{1,0:T(8,128)(2,1)}), bf16[1024,768]{1,0:T(8,128)(2,1)}) %all-gather.36.cloned.1.call-update) | async-done | bytes 1572880 | tf_op jit(solution)/shard_map/all_gather | solution.py:127
  383.5 16.3 %all-gather.38.cloned.1.call-done = bf16[1024,768]{1,0:T(8,128)(2,1)} async-done(((bf16[128,768]{1,0:T(8,128)(2,1)}), bf16[1024,768]{1,0:T(8,128)(2,1)}) %all-gather.38.cloned.1.call-update) | async-done | bytes 1572880 | tf_op jit(solution)/shard_map/all_gather | solution.py:128
  518.9 13.9 %all-gather = f32[1,1024,12]{1,2,0:T(8,128)S(1)} all-gather(f32[1,128,12]{1,2,0:T(8,128)S(1)} %get-tuple-element.573), channel_id=2, replica_groups=mesh['section'=2,'ctx'=8,'wshard'=2] {'ctx'}, dimensions={1}, use_global_device_ids=true | all-gather | bytes 55296 | tf_op jit(solution)/shard_map/all_gather | solution.py:198
  533.6 14.2 %all_gather.87 = f32[1024,12]{0,1:T(8,128)S(1)} all-gather(f32[128,12]{0,1:T(8,128)S(1)} %multiply_reduce_fusion.21), channel_id=1, replica_groups=mesh['section'=2,'ctx'=8,'wshard'=2] {'ctx'}, dimensions={0}, use_global_device_ids=true | all-gather | bytes 55296 | tf_op jit(solution)/shard_map/all_gather | solution.py:199
  564.3 34.8 %while.39 = (s32[]{:T(128)}, f32[128,12,64]{0,2,1:T(8,128)}, f32[128,12,64]{0,2,1:T(8,128)}, bf16[2,512,768]{2,1,0:T(8,128)(2,1)}, bf16[128,12,64]{0,2,1:T(8,128...) while((s32[]{:T(128)}, f32[128,12,64]{0,2,1:T(8,128)}, ...), condition=%wide.region_24.25_spmd.clone, body=%wide.region_23.24_spmd.clone.sunk | while | flops 409436160 | bytes 21110920 | solution.py:240
  609.6 14.2 %all-gather.1 = f32[1,1024,12]{1,2,0:T(8,128)S(1)} all-gather(f32[1,128,12]{1,2,0:T(8,128)S(1)} %copy-done.171), channel_id=3, replica_groups=mesh['section'=2,'ctx'=8,'wshard'=2] {'ctx'}, dimensions={1}, use_global_device_ids=true | all-gather | bytes 55296 | tf_op jit(solution)/shard_map/all_gather | solution.py:198
  630.8 14.1 %all-gather.2 = f32[1,1024,12]{1,2,0:T(8,128)S(1)} all-gather(f32[1,128,12]{1,2,0:T(8,128)S(1)} %get-tuple-element.571), channel_id=4, replica_groups=mesh['section'=2,'ctx'=8,'wshard'=2] {'ctx'}, dimensions={1}, use_global_device_ids=true | all-gather | bytes 55296 | tf_op jit(solution)/shard_map/all_gather | solution.py:198
  660.3 14.4 %all_gather.91 = f32[1024,12]{0,1:T(8,128)S(1)} all-gather(f32[128,12]{0,1:T(8,128)S(1)} %multiply_reduce_fusion.16), channel_id=1, replica_groups=mesh['section'=2,'ctx'=8,'wshard'=2] {'ctx'}, dimensions={0}, use_global_device_ids=true | all-gather | bytes 55296 | tf_op jit(solution)/shard_map/all_gather | solution.py:199
  682.1 34.9 %while.40 = (s32[]{:T(128)}, f32[128,12,64]{0,2,1:T(8,128)}, f32[128,12,64]{0,2,1:T(8,128)}, bf16[2,512,768]{2,1,0:T(8,128)(2,1)}, bf16[128,12,64]{0,2,1:T(8,128...) while((s32[]{:T(128)}, f32[128,12,64]{0,2,1:T(8,128)}, ...), condition=%wide.region_35.36_spmd.clone, body=%wide.region_34.35_spmd.clone.sunk | while | flops 409436160 | bytes 21110920 | solution.py:240
  751.6 14.1 %all_gather.95 = f32[1024,12]{0,1:T(8,128)S(1)} all-gather(f32[128,12]{0,1:T(8,128)S(1)} %multiply_reduce_fusion.11), channel_id=1, replica_groups=mesh['section'=2,'ctx'=8,'wshard'=2] {'ctx'}, dimensions={0}, use_global_device_ids=true | all-gather | bytes 55296 | tf_op jit(solution)/shard_map/all_gather | solution.py:199
  774.9 34.6 %while.41 = (s32[]{:T(128)}, f32[128,12,64]{0,2,1:T(8,128)}, f32[128,12,64]{0,2,1:T(8,128)S(1)}, bf16[2,512,768]{2,1,0:T(8,128)(2,1)}, bf16[128,12,64]{0,2,1:T(8...) while((s32[]{:T(128)}, f32[128,12,64]{0,2,1:T(8,128)}, ...), condition=%wide.region_46.47_spmd.clone, body=%wide.region_45.46_spmd.clone.sunk | while | flops 409436160 | bytes 21110920 | solution.py:240
  853.0 33.7 %reduce-scatter.19.cloned.1.call-done = f32[48,1]{1,0:T(8,128)} async-done(((f32[768,1]{1,0:T(8,128)}), f32[48,1]{1,0:T(8,128)}) %reduce-scatter.19.cloned.1.call-update) | async-done | bytes 208
  888.0 65.0 %reduce-scatter.13.cloned.1.call-done = f32[1,48,768]{2,1,0:T(8,128)} async-done(((f32[1,768,768]{2,1,0:T(8,128)}), f32[1,48,768]{2,1,0:T(8,128)}) %reduce-scatter.13.cloned.1.call-update) | async-done | bytes 147472 | tf_op jit(solution)/shard_map/reduce_scatter | solution.py:356
  953.1 71.9 %reduce-scatter.17.cloned.1.call-done = f32[1,72,768]{2,1,0:T(8,128)} async-done(((f32[1,1152,768]{2,1,0:T(8,128)}), f32[1,72,768]{2,1,0:T(8,128)}) %reduce-scatter.17.cloned.1.call-update) | async-done | bytes 221200 | tf_op jit(solution)/shard_map/reduce_scatter | solution.py:359
  1024.9 94.1 %reduce-scatter.15.cloned.1.call-done = f32[1,48,2304]{2,1,0:T(8,128)} async-done(((f32[1,768,2304]{2,1,0:T(8,128)}), f32[1,48,2304]{2,1,0:T(8,128)}) %reduce-scatter.15.cloned.1.call-update) | async-done | bytes 442384 | tf_op jit(solution)/shard_map/reduce_scatter | solution.py:358
  1119.0 94.2 %reduce-scatter.11.cloned.1.call-done = f32[1,48,2304]{2,1,0:T(8,128)} async-done(((f32[1,768,2304]{2,1,0:T(8,128)}), f32[1,48,2304]{2,1,0:T(8,128)}) %reduce-scatter.11.cloned.1.call-update) | async-done | bytes 442384 | tf_op jit(solution)/shard_map/reduce_scatter | solution.py:355
  (864 shorter events, 496.6 us)
Async XLA Ops:
  7.2 52.8 %all-gather.20.cloned.1.call-start = ((), (), s32[]{:S(2)}) async-start(), calls=%async_computation.6 | async-start | bytes 3760128 | tf_op jit(solution)/shard_map/all_gather | solution.py:283
  7.9 80.3 %all-gather.22.cloned.1.call-start = ((), (), s32[]{:S(2)}) async-start(), calls=%async_computation.7 | async-start | bytes 1769472 | tf_op jit(solution)/shard_map/all_gather | solution.py:127
  64.0 51.1 %all-gather.24.cloned.1.call-start = ((), (), s32[]{:S(2)}) async-start(), calls=%async_computation.8 | async-start | bytes 1769472 | tf_op jit(solution)/shard_map/all_gather | solution.py:128
  64.7 90.4 %all-gather.26.cloned.1.call-start = ((), (), s32[]{:S(2)}) async-start(), calls=%async_computation.9 | async-start | bytes 1253376 | tf_op jit(solution)/shard_map/all_gather | solution.py:284
  65.3 138.2 %all-gather.28.cloned.1.call-start = ((), (), s32[]{:S(2)}) async-start(), calls=%async_computation.10 | async-start | bytes 3760128 | tf_op jit(solution)/shard_map/all_gather | solution.py:286
  65.9 179.1 %all-gather.30.cloned.1.call-start = ((), (), s32[]{:S(2)}) async-start(), calls=%async_computation.11 | async-start | bytes 1880064 | tf_op jit(solution)/shard_map/all_gather | solution.py:287
  66.5 223.1 %all-gather.32.cloned.1.call-start = ((), (), s32[]{:S(2)}) async-start(), calls=%async_computation.12 | async-start | bytes 1769472 | tf_op jit(solution)/shard_map/all_gather | solution.py:127
  265.3 50.5 %all-gather.34.cloned.1.call-start = ((), (), s32[]{:S(2)}) async-start(), calls=%async_computation.13 | async-start | bytes 1769472 | tf_op jit(solution)/shard_map/all_gather | solution.py:128
  266.0 107.7 %all-gather.36.cloned.1.call-start = ((), (), s32[]{:S(2)}) async-start(), calls=%async_computation.14 | async-start | bytes 1769472 | tf_op jit(solution)/shard_map/all_gather | solution.py:127
  347.9 51.9 %all-gather.38.cloned.1.call-start = ((), (), s32[]{:S(2)}) async-start(), calls=%async_computation.15 | async-start | bytes 1769472 | tf_op jit(solution)/shard_map/all_gather | solution.py:128
  349.7 212.0 %all-gather.40.cloned.1.call-start = ((), (), s32[]{:S(2)}) async-start(), calls=%async_computation.16 | async-start | bytes 1769472 | tf_op jit(solution)/shard_map/all_gather | solution.py:215
  358.1 206.2 %all-gather.42.cloned.1.call-start = ((), (), s32[]{:S(2)}) async-start(), calls=%async_computation.17 | async-start | bytes 1769472 | tf_op jit(solution)/shard_map/all_gather | solution.py:216
  428.4 219.0 %all-gather.44.cloned.1.call-start = ((), (), s32[]{:S(2)}) async-start(), calls=%async_computation.18 | async-start | bytes 1769472 | tf_op jit(solution)/shard_map/all_gather | solution.py:215
  438.8 211.2 %all-gather.48.cloned.1.call-start = ((), (), s32[]{:S(2)}) async-start(), calls=%async_computation.20 | async-start | bytes 1769472 | tf_op jit(solution)/shard_map/all_gather | solution.py:215
  486.7 195.4 %all-gather.46.cloned.1.call-start = ((), (), s32[]{:S(2)}) async-start(), calls=%async_computation.19 | async-start | bytes 1769472 | tf_op jit(solution)/shard_map/all_gather | solution.py:216
  607.3 16.4 %collective-permute-start.2 = (bf16[128,768]{1,0:T(8,128)(2,1)S(1)}, bf16[128,768]{1,0:T(8,128)(2,1)S(1)}, u32[]{:S(2)}, u32[]{:S(2)}) collective-permute-start(bf16[128,768]{1,0:T(8,128)(2,1)S(1)} %get-tuple-element.469), channel_id=1, source_target_pairs={{16,0},{17,1},{18,2},{19,3},{20,4},{21,5},{22,6},{23,7},{24,8},{25... | collective-permute-start | bytes 589832 | tf_op jit(solution)/shard_map/ppermute | solution.py:19
  630.8 144.1 %all-gather.50.cloned.1.call-start = ((), (), s32[]{:S(2)}) async-start(), calls=%async_computation.21 | async-start | bytes 1769472 | tf_op jit(solution)/shard_map/all_gather | solution.py:216
  725.4 9.2 collective-permute-start.3
  741.5 108.6 %reduce-scatter.21.cloned.1.call-start = ((), (), s32[]{:S(2)}) async-start(), calls=%async_computation.27 | async-start | bytes 417792
  773.9 112.8 %reduce-scatter.19.cloned.1.call-start = ((), (), s32[]{:S(2)}) async-start(), calls=%async_computation.26 | async-start | bytes 417792
  817.5 135.5 %reduce-scatter.13.cloned.1.call-start = ((), (), s32[]{:S(2)}) async-start(), calls=%async_computation.23 | async-start | bytes 2506752 | tf_op jit(solution)/shard_map/reduce_scatter | solution.py:356
  821.2 203.7 %reduce-scatter.17.cloned.1.call-start = ((), (), s32[]{:S(2)}) async-start(), calls=%async_computation.25 | async-start | bytes 3760128 | tf_op jit(solution)/shard_map/reduce_scatter | solution.py:359
  828.4 290.7 %reduce-scatter.15.cloned.1.call-start = ((), (), s32[]{:S(2)}) async-start(), calls=%async_computation.24 | async-start | bytes 7520256 | tf_op jit(solution)/shard_map/reduce_scatter | solution.py:358
  836.7 376.5 %reduce-scatter.11.cloned.1.call-start = ((), (), s32[]{:S(2)}) async-start(), calls=%async_computation.22 | async-start | bytes 7520256 | tf_op jit(solution)/shard_map/reduce_scatter | solution.py:355
  (215 other events, 1325.0 us)
Sparse Core Ops, SparseCore 0:
  10.3 49.6 all-gather.19
  64.1 24.0 all-gather.21
  90.4 24.5 all-gather.23
  117.2 37.9 all-gather.25
  157.2 46.2 all-gather.27
  205.6 39.3 all-gather.29
  265.4 24.0 all-gather.31
  291.2 24.5 all-gather.33
  348.0 25.6 all-gather.35
  375.2 24.5 all-gather.37
  401.4 26.6 all-gather.39
  429.6 24.2 all-gather.41
  455.5 26.6 all-gather.43
  486.8 25.7 all-gather.47
  630.9 25.7 all-gather.45
  741.7 24.2 all-gather.49
  774.0 54.2 reduce-scatter.20
  832.1 54.5 reduce-scatter.18
  891.0 61.9 reduce-scatter.12
  957.9 67.0 reduce-scatter.16
  1030.1 88.9 reduce-scatter.14
  1123.6 89.5 reduce-scatter.10
where the time goes:
time: 1230 us; the launch traced here: 1220 us
  waiting for transfers between devices  598 us (49%)
  local copies, waits for them, and re-layouts  197 us (16%)
  matrix products  190 us (15%)
  blocking collectives  120 us (10%)
  other arithmetic  78.9 us (6%)
  between operations  22.5 us (2%)
  starting transfers between devices  13 us (1%)
    reduce_scatter x1, waiting for transfers between devices, body(): lax.psum_scatter(raised[1], ('ctx', 'wshard'), scatter_dimension=1, tiled...  94.2 us
    reduce_scatter x1, waiting for transfers between devices, body(): lax.psum_scatter(raised[4], ('ctx', 'wshard'), scatter_dimension=1, tiled...  94.1 us
    reduce_scatter x1, waiting for transfers between devices, body(): lax.psum_scatter(raised[5], ('ctx', 'wshard'), scatter_dimension=1, tiled...  71.9 us
    reduce_scatter x1, waiting for transfers between devices, body(): lax.psum_scatter(raised[2], ('ctx', 'wshard'), scatter_dimension=1, tiled...  65 us
    all_gather x3, waiting for transfers between devices, forward_layer(): lax.all_gather(value_rows, 'ctx', axis=0, tiled=True)  58.5 us
    all_gather x3, waiting for transfers between devices, forward_layer(): lax.all_gather(key_rows, 'ctx', axis=0, tiled=True)  49.5 us
    dynamic_slice x36, local copies, waits for them, and re-layouts, backward_layer(): lax.scan(query_block, (empty_heads, empty_heads), stacked)  47.8 us
    all_gather x1, waiting for transfers between devices, body(): lax.all_gather(in_weight, ('ctx', 'wshard'), axis=1, tiled=True)  45.8 us
  transfers between devices with their start and end apart: 26, of which 17 were waited for; matrix products, arithmetic and copies ran while one was open for 30% of the time, Pallas kernels for 0%

commit v1 on v0

--- a/solution.py
+++ b/solution.py
@@ -1,6 +1,8 @@
 import jax
 import jax.numpy as jnp
 from jax import lax
+from jax.experimental import pallas as pl
+from jax.experimental.pallas import tpu as pltpu
 from jax.sharding import PartitionSpec as P
 
 D = 768
@@ -123,10 +125,10 @@
         jnp.zeros((HEADS, tok_rows), jnp.float32),
         jnp.zeros((tok_rows, HEADS, HEAD_DIM), jnp.float32),
     )
-    key_rows, value_rows = (
-        lax.all_gather(key_rows, "ctx", axis=0, tiled=True),
-        lax.all_gather(value_rows, "ctx", axis=0, tiled=True),
-    )
+    both_rows = lax.all_gather(
+        jnp.concatenate([key_rows, value_rows], axis=-1), "ctx", axis=0, tiled=True
+    )
+    key_rows, value_rows = both_rows[:, :D], both_rows[:, D:]
     final_state = absorb(start_state, (key_rows, value_rows), query_heads)
     largest, running_sum, weighted = final_state
     attended = join_heads(weighted / running_sum.T[:, :, None])
@@ -194,10 +196,22 @@
         )
     )
     deltas = jnp.sum(grad_attended.astype(jnp.float32) * split_heads(attended), axis=-1)
-    all_logs, all_deltas = (
-        lax.all_gather(log_sums, "ctx", axis=0, tiled=True),
-        lax.all_gather(deltas, "ctx", axis=0, tiled=True),
-    )
+    stats = jnp.concatenate([log_sums, deltas], axis=-1)
+    stats_high = lax.reduce_precision(stats, 8, 7)
+    packed = jnp.concatenate(
+        [
+            join_heads(query_heads),
+            join_heads(grad_attended),
+            stats_high.astype(jnp.bfloat16),
+            (stats - stats_high).astype(jnp.bfloat16),
+        ],
+        axis=-1,
+    )
+    packed = lax.all_gather(packed, "ctx", axis=0, tiled=True)
+    queries_all, grads_all = packed[:, :D], packed[:, D : 2 * D]
+    stats_all = packed[:, 2 * D :].astype(jnp.float32)
+    stats_all = stats_all[:, : 2 * HEADS] + stats_all[:, 2 * HEADS :]
+    all_logs, all_deltas = stats_all[:, :HEADS], stats_all[:, HEADS:]
     empty_heads = jnp.zeros((tok_rows, HEADS, HEAD_DIM), jnp.float32)
     key_heads = split_heads(key_rows)
     value_heads = split_heads(value_rows)
@@ -211,12 +225,8 @@
     own_start = cycle_place * tok_rows
     own_keys = split_heads(lax.dynamic_slice_in_dim(key_rows, own_start, tok_rows, 0))
     own_values = split_heads(lax.dynamic_slice_in_dim(value_rows, own_start, tok_rows, 0))
-    queries_all, grads_all = (
-        lax.all_gather(join_heads(query_heads), "ctx", axis=0, tiled=True),
-        lax.all_gather(join_heads(grad_attended), "ctx", axis=0, tiled=True),
-    )
     total_rows = queries_all.shape[0]
-    block_rows = min(512, total_rows)
+    block_rows = min(1024, total_rows)
     block_count = total_rows // block_rows
 
     def query_block(running, pieces):
@@ -237,7 +247,17 @@
         all_logs.reshape(block_count, block_rows, HEADS),
         all_deltas.reshape(block_count, block_rows, HEADS),
     )
-    (grad_key, grad_value_heads), _ = lax.scan(query_block, (empty_heads, empty_heads), stacked)
+    if block_count == 1:
+        grad_key, grad_value_heads = key_value_terms(
+            split_heads(queries_all),
+            split_heads(grads_all),
+            all_logs,
+            all_deltas,
+            own_keys,
+            own_values,
+        )
+    else:
+        (grad_key, grad_value_heads), _ = lax.scan(query_block, (empty_heads, empty_heads), stacked)
     grad_value = join_heads(grad_value_heads)
     query_grad_raw = grad_query * cosine + rotate_back(grad_query * sine)
     key_grad_raw = grad_key * cosine + rotate_back(grad_key * sine)
@@ -266,6 +286,240 @@
         buffer, jnp.where(is_valid, value, previous), batch_slot, 0
     )
 
+MESH = pl.DeviceIdType.MESH
+
+
+def greet(chips):
+    me = lax.axis_index("ctx")
+    chip, core = me // 2, me % 2
+    w = lax.axis_index("wshard")
+    barrier = pltpu.get_barrier_semaphore()
+    peers = [{"ctx": ((chip + d) % chips) * 2 + core} for d in range(1, chips)]
+    peers += [{"wshard": 1 - w}, {"ctx": chip * 2 + 1 - core}]
+    for peer in peers:
+        pl.semaphore_signal(barrier, inc=1, device_id=peer, device_id_type=MESH)
+    pl.semaphore_wait(barrier, len(peers))
+
+
+def gather_kernel(chips, count, *refs):
+    ins, outs = refs[:count], refs[count : 2 * count]
+    own_sem, z_send, z_recv, y_send, y_recv, c_send, c_recv = refs[2 * count :]
+    me = lax.axis_index("ctx")
+    chip, core = me // 2, me % 2
+    w = lax.axis_index("wshard")
+
+    def slot(chip_at, core_at, w_at):
+        return (chip_at * 2 + core_at) * 2 + w_at
+
+    greet(chips)
+    own = slot(chip, core, w)
+
+    def to_chip(a, d):
+        return pltpu.make_async_remote_copy(
+            ins[a].at[0], outs[a].at[own], z_send.at[a, d - 1], z_recv.at[a, d - 1],
+            device_id={"ctx": ((chip + d) % chips) * 2 + core}, device_id_type=MESH)
+
+    def to_wide(a, d):
+        at = slot((chip - d + chips) % chips, core, w)
+        source = ins[a].at[0] if d == 0 else outs[a].at[at]
+        return pltpu.make_async_remote_copy(
+            source, outs[a].at[at], y_send.at[a, d], y_recv.at[a, d],
+            device_id={"wshard": 1 - w}, device_id_type=MESH)
+
+    def to_core(a, d, far):
+        at = slot((chip - d + chips) % chips, core, 1 - w if far else w)
+        source = ins[a].at[0] if d == 0 and not far else outs[a].at[at]
+        index = d + chips * far
+        return pltpu.make_async_remote_copy(
+            source, outs[a].at[at], c_send.at[a, index], c_recv.at[a, index],
+            device_id={"ctx": chip * 2 + 1 - core}, device_id_type=MESH)
+
+    def keep(a):
+        return pltpu.make_async_copy(ins[a].at[0], outs[a].at[own], own_sem.at[a])
+
+    for a in range(count):
+        to_wide(a, 0).start()
+        for d in range(1, chips):
+            to_chip(a, d).start()
+        to_core(a, 0, 0).start()
+        keep(a).start()
+    for a in range(count):
+        for d in range(1, chips):
+            to_chip(a, d).wait_recv()
+            to_wide(a, d).start()
+            to_core(a, d, 0).start()
+        for d in range(chips):
+            to_wide(a, d).wait_recv()
+            to_core(a, d, 1).start()
+    for a in range(count):
+        keep(a).wait()
+        for d in range(chips):
+            for far in range(2):
+                to_core(a, d, far).wait_recv()
+    for a in range(count):
+        for d in range(1, chips):
+            to_chip(a, d).wait_send()
+        for d in range(chips):
+            to_wide(a, d).wait_send()
+            for far in range(2):
+                to_core(a, d, far).wait_send()
+
+
+def gather_shards(arrays, chips):
+    count = len(arrays)
+    shards = chips * 4
+    return pl.pallas_call(
+        lambda *refs: gather_kernel(chips, count, *refs),
+        out_shape=[jax.ShapeDtypeStruct((shards,) + x.shape[1:], x.dtype) for x in arrays],
+        in_specs=[pl.BlockSpec(memory_space=pl.ANY)] * count,
+        out_specs=[pl.BlockSpec(memory_space=pl.ANY)] * count,
+        scratch_shapes=[
+            pltpu.SemaphoreType.DMA((count,)),
+            pltpu.SemaphoreType.DMA((count, chips - 1)),
+            pltpu.SemaphoreType.DMA((count, chips - 1)),
+            pltpu.SemaphoreType.DMA((count, chips)),
+            pltpu.SemaphoreType.DMA((count, chips)),
+            pltpu.SemaphoreType.DMA((count, 2 * chips)),
+            pltpu.SemaphoreType.DMA((count, 2 * chips)),
+        ],
+        compiler_params=pltpu.CompilerParams(collective_id=0, has_side_effects=True),
+        name="gather_shards",
+    )(*arrays)
+
+
+def scatter_kernel(chips, count, *refs):
+    ins, outs = refs[:count], refs[count : 2 * count]
+    rest = refs[2 * count :]
+    from_core, from_wide, from_chip = rest[:count], rest[count : 2 * count], rest[2 * count : 3 * count]
+    half, near = rest[3 * count : 4 * count], rest[4 * count : 5 * count]
+    c_send, c_recv, y_send, y_recv, z_send, z_recv = rest[5 * count :]
+    me = lax.axis_index("ctx")
+    chip, core = me // 2, me % 2
+    w = lax.axis_index("wshard")
+
+    def slot(chip_at, core_at, w_at):
+        return (chip_at * 2 + core_at) * 2 + w_at
+
+    def wide(value):
+        return value.astype(jnp.float32)
+
+    greet(chips)
+
+    def to_core(a, d, far):
+        at = slot((chip + d) % chips, 1 - core, 1 - w if far else w)
+        return pltpu.make_async_remote_copy(
+            ins[a].at[at], from_core[a].at[d, far], c_send.at[a, d, far], c_recv.at[a, d, far],
+            device_id={"ctx": chip * 2 + 1 - core}, device_id_type=MESH)
+
+    def to_wide(a, d):
+        return pltpu.make_async_remote_copy(
+            half[a].at[d], from_wide[a].at[d], y_send.at[a, d], y_recv.at[a, d],
+            device_id={"wshard": 1 - w}, device_id_type=MESH)
+
+    def to_chip(a, d):
+        return pltpu.make_async_remote_copy(
+            near[a].at[d - 1], from_chip[a].at[d - 1], z_send.at[a, d - 1], z_recv.at[a, d - 1],
+            device_id={"ctx": ((chip + d) % chips) * 2 + core}, device_id_type=MESH)
+
+    order = list(range(1, chips)) + [0]
+    for far in (1, 0):
+        for a in range(count):
+            for d in order:
+                to_core(a, d, far).start()
+    for a in range(count):
+        for d in order:
+            to_core(a, d, 1).wait_recv()
+            mine = ins[a][slot((chip + d) % chips, core, 1 - w)]
+            half[a][d] = (wide(mine) + wide(from_core[a][d, 1])).astype(jnp.bfloat16)
+            to_wide(a, d).start()
+    for a in range(count):
+        for d in order:
+            to_core(a, d, 0).wait_recv()
+            to_wide(a, d).wait_recv()
+            mine = ins[a][slot((chip + d) % chips, core, w)]
+            total = wide(mine) + wide(from_core[a][d, 0]) + wide(from_wide[a][d])
+            if d == 0:
+                outs[a][0] = total
+            else:
+                near[a][d - 1] = total.astype(jnp.bfloat16)
+                to_chip(a, d).start()
+    for a in range(count):
+        total = outs[a][0]
+        for d in range(1, chips):
+            to_chip(a, d).wait_recv()
+            total = total + wide(from_chip[a][d - 1])
+        outs[a][0] = total
+    for a in range(count):
+        for d in range(chips):
+            to_core(a, d, 0).wait_send()
+            to_core(a, d, 1).wait_send()
+            to_wide(a, d).wait_send()
+            if d:
+                to_chip(a, d).wait_send()
+
+
+def scatter_sums(arrays, chips):
+    count = len(arrays)
+    tails = [x.shape[1:] for x in arrays]
+
+    def slots(*lead):
+        return [pltpu.VMEM(lead + tail, jnp.bfloat16) for tail in tails]
+
+    return pl.pallas_call(
+        lambda *refs: scatter_kernel(chips, count, *refs),
+        out_shape=[jax.ShapeDtypeStruct((1,) + tail, jnp.float32) for tail in tails],
+        in_specs=[pl.BlockSpec(memory_space=pltpu.VMEM)] * count,
+        out_specs=[pl.BlockSpec(memory_space=pltpu.VMEM)] * count,
+        scratch_shapes=slots(chips, 2) + slots(chips) + slots(chips - 1) + slots(chips) + slots(chips - 1)
+        + [
+            pltpu.SemaphoreType.DMA((count, chips, 2)),
+            pltpu.SemaphoreType.DMA((count, chips, 2)),
+            pltpu.SemaphoreType.DMA((count, chips)),
+            pltpu.SemaphoreType.DMA((count, chips)),
+            pltpu.SemaphoreType.DMA((count, chips - 1)),
+            pltpu.SemaphoreType.DMA((count, chips - 1)),
+        ],
+        compiler_params=pltpu.CompilerParams(
+            collective_id=1, has_side_effects=True, vmem_limit_bytes=48 * 1024 * 1024
+        ),
+        name="scatter_sums",
+    )(*arrays)
+
+
+def use_kernels():
+    cycle, wides = lax.axis_size("ctx"), lax.axis_size("wshard")
+    return wides == 2 and cycle % 2 == 0 and 4 <= cycle <= 8
+
+
+def gather_params(attn_gain, qkv_weight, out_weight, mlp_gain, in_weight, down_weight):
+    chips = lax.axis_size("ctx") // 2
+    gain_width = attn_gain.shape[1]
+    gains = jnp.concatenate([attn_gain, mlp_gain], axis=0)
+    gains = jnp.pad(gains, ((0, 14), (0, 128 - gain_width)))[None]
+    gains, qkv, out, into, down = gather_shards(
+        (gains, qkv_weight, out_weight, in_weight, down_weight), chips
+    )
+    return (
+        gains[:, 0, :gain_width].reshape(D),
+        qkv.reshape(D, -1),
+        out.reshape(D, -1),
+        gains[:, 1, :gain_width].reshape(D),
+        into.reshape(D, -1),
+        down.reshape(-1, D),
+    )
+
+
+def scatter_grads(summed):
+    shards = lax.axis_size("ctx") * 2
+    gain_one, qkv, out, gain_two, into, down = summed
+    gain_width = gain_one.shape[0] // shards
+    gains = jnp.stack([gain_one.reshape(shards, gain_width), gain_two.reshape(shards, gain_width)], axis=1)
+    gains = jnp.pad(gains, ((0, 0), (0, 14), (0, 128 - gain_width)))
+    parts = [x.reshape(shards, x.shape[0] // shards, x.shape[1]) for x in (down, into, out, qkv)]
+    parts = [x.astype(jnp.bfloat16) for x in [gains] + parts]
+    gains, down, into, out, qkv = scatter_sums(parts, shards // 4)
+    return (gains[:, 0, :gain_width], qkv, out, gains[:, 1, :gain_width], into, down)
+
 
 def body(
     tokens,
@@ -278,15 +532,20 @@
     in_weight,
     down_weight,
 ):
-    gathered = (
-        lax.all_gather(attn_gain, ("ctx", "wshard"), axis=1, tiled=True),
-        lax.all_gather(qkv_weight, ("ctx", "wshard"), axis=1, tiled=True),
-        lax.all_gather(out_weight, ("ctx", "wshard"), axis=1, tiled=True),
-        lax.all_gather(mlp_gain, ("ctx", "wshard"), axis=1, tiled=True),
-        lax.all_gather(in_weight, ("ctx", "wshard"), axis=1, tiled=True),
-        lax.all_gather(down_weight, ("ctx", "wshard"), axis=1, tiled=True),
-    )
-    params = tuple((whole[0] for whole in gathered))
+    if use_kernels():
+        params = gather_params(
+            attn_gain, qkv_weight, out_weight, mlp_gain, in_weight, down_weight
+        )
+    else:
+        gathered = (
+            lax.all_gather(attn_gain, ("ctx", "wshard"), axis=1, tiled=True),
+            lax.all_gather(qkv_weight, ("ctx", "wshard"), axis=1, tiled=True),
+            lax.all_gather(out_weight, ("ctx", "wshard"), axis=1, tiled=True),
+            lax.all_gather(mlp_gain, ("ctx", "wshard"), axis=1, tiled=True),
+            lax.all_gather(in_weight, ("ctx", "wshard"), axis=1, tiled=True),
+            lax.all_gather(down_weight, ("ctx", "wshard"), axis=1, tiled=True),
+        )
+        params = tuple((whole[0] for whole in gathered))
     section_id = lax.axis_index("section")
     section_count = lax.axis_size("section")
     cycle_place = lax.axis_index("ctx")
@@ -349,15 +608,18 @@
             else tuple((left + right for left, right in zip(summed, weight_grads)))
         )
         grad_received = shifted(outgoing, "section", -1)
-    raised = [grad_term[None] for grad_term in summed]
-    summed = (
-        lax.psum_scatter(raised[0], ("ctx", "wshard"), scatter_dimension=1, tiled=True),
-        lax.psum_scatter(raised[1], ("ctx", "wshard"), scatter_dimension=1, tiled=True),
-        lax.psum_scatter(raised[2], ("ctx", "wshard"), scatter_dimension=1, tiled=True),
-        lax.psum_scatter(raised[3], ("ctx", "wshard"), scatter_dimension=1, tiled=True),
-        lax.psum_scatter(raised[4], ("ctx", "wshard"), scatter_dimension=1, tiled=True),
-        lax.psum_scatter(raised[5], ("ctx", "wshard"), scatter_dimension=1, tiled=True),
-    )
+    if use_kernels():
+        summed = scatter_grads(summed)
+    else:
+        raised = [grad_term[None] for grad_term in summed]
+        summed = (
+            lax.psum_scatter(raised[0], ("ctx", "wshard"), scatter_dimension=1, tiled=True),
+            lax.psum_scatter(raised[1], ("ctx", "wshard"), scatter_dimension=1, tiled=True),
+            lax.psum_scatter(raised[2], ("ctx", "wshard"), scatter_dimension=1, tiled=True),
+            lax.psum_scatter(raised[3], ("ctx", "wshard"), scatter_dimension=1, tiled=True),
+            lax.psum_scatter(raised[4], ("ctx", "wshard"), scatter_dimension=1, tiled=True),
+            lax.psum_scatter(raised[5], ("ctx", "wshard"), scatter_dimension=1, tiled=True),
+        )
     return (
         section_outs[None, :, None],
         input_grads[None, :, None],

time: 1230 us -> 790 us (0.64)
  waiting for transfers between devices: 598 us -> 80.8 us
  Pallas kernels: 0 us -> 144 us
  blocking collectives: 120 us -> 0 us
  other arithmetic: 78.9 us -> 109 us
  local copies, waits for them, and re-layouts: 197 us -> 216 us
    reduce_scatter x4 -> x0, waiting for transfers between devices: 325 us -> none  [the longest x1 94.2 us: body(): lax.psum_scatter(raised[1], ('ctx', 'wshard'), scatter_dimension=1, tiled...]
    all_gather x16 -> x6, waiting for transfers between devices: 227 us -> 62.9 us  [the longest x3 40.4 us: forward_layer(): lax.all_gather(jnp.concatenate([key_rows, value_rows], axis=-1), 'ctx', a...]
    pallas_call x0 -> x2, Pallas kernels: none -> 144 us  [the longest x1 74.6 us: gather_shards(): pl.pallas_call(lambda *refs: gather_kernel(chips, count, *refs), out_shap...]
    all_gather x6 -> x0, blocking collectives: 84.8 us -> none  [the longest x3 42.6 us: backward_layer(): lax.all_gather(deltas, 'ctx', axis=0, tiled=True)]
    dynamic_slice x37 -> x0, local copies, waits for them, and re-layouts: 48.8 us -> none  [the longest x36 47.8 us: backward_layer(): lax.scan(query_block, (empty_heads, empty_heads), stacked)]
    slice x0 -> x15, local copies, waits for them, and re-layouts: none -> 38.2 us  [the longest x9 23.4 us: backward_layer(): queries_all, grads_all = (packed[:, :D], packed[:, D:2 * D])]
    unnamed x24 -> x6, waiting for transfers between devices: 36.2 us -> 0.1 us
    unnamed x1 -> x0, blocking collectives: 35.4 us -> none
  transfers between devices with their start and end apart: 26 -> 10, of which waited for: 17 -> 8; matrix products, arithmetic and copies ran while one was open for 30% -> 23% of each run, Pallas kernels for 0% -> 0%
where the time goes in v1:
time: 790 us; the launch traced here: 777 us
  local copies, waits for them, and re-layouts  216 us (27%)
  matrix products  194 us (25%)
  Pallas kernels  144 us (18%)
  other arithmetic  109 us (14%)
  waiting for transfers between devices  80.8 us (10%)
  between operations  20.9 us (3%)
  starting transfers between devices  11.4 us (1%)
    pallas_call x1, Pallas kernels, gather_shards(): pl.pallas_call(lambda *refs: gather_kernel(chips, count, *refs), out_shap...  74.6 us
    pallas_call x1, Pallas kernels, scatter_sums(): pl.pallas_call(lambda *refs: scatter_kernel(chips, count, *refs), out_sha...  69.7 us
    all_gather x3, waiting for transfers between devices, forward_layer(): lax.all_gather(jnp.concatenate([key_rows, value_rows], axis=-1), 'ctx', a...  40.4 us
    dynamic_slice x23, local copies, waits for them, and re-layouts, keep_slot(): previous = lax.dynamic_index_in_dim(buffer, batch_slot, 0, keepdims=False)  37.5 us
    unnamed x426, local copies, waits for them, and re-layouts  29 us
    dot_general x3, matrix products, key_value_terms(): jnp.einsum('hqk,qhe->khe', grad_scores, query_heads, preferred_element_ty...  26.5 us
    broadcast_in_dim x13, local copies, waits for them, and re-layouts, keep_slot(): lax.dynamic_update_index_in_dim(buffer, jnp.where(is_valid, value, previo...  25.7 us
    slice x9, local copies, waits for them, and re-layouts, backward_layer(): queries_all, grads_all = (packed[:, :D], packed[:, D:2 * D])  23.4 us
  transfers between devices with their start and end apart: 10, of which 8 were waited for; matrix products, arithmetic and copies ran while one was open for 23% of the time, Pallas kernels for 0%

profile of v1, /device:TPU:0, one launch (start us, length us, event | category | flops | bytes accessed | tf_op | source)
XLA Modules:
  0.0 776.6 jit_solution(10440823783588722374)
XLA Ops:
  8.5 74.6 %gather_shards.1 = (bf16[16,16,128]{2,1,0:T(8,128)(2,1)}, bf16[16,48,2304]{2,1,0:T(8,128)(2,1)}, bf16[16,48,768]{2,1,0:T(8,128)(2,1)}, bf16[16,48,2304]{2,1,0:T(8,128)(2,1)}, bf16[16,72,768]{2,1,0:T(8,128)(2,1)}) custom-call(bf16[1,16,128]{2,1,0:T(8,128)(2,1)} %fusion.438.refs_0_, bf16[1,48,2304]{2,1,0:T(8,128)(2,1)} %refs_1_.1, ...), custom_call_target="tpu_custom_call" | custom-call | tf_op jit(solution)/shard_map/gather_shards/pallas_call | solution.py:371
  100.3 38.0 %all-gather.7.cloned.1.call-done = bf16[1024,1536]{1,0:T(8,128)(2,1)} async-done(((bf16[128,1536]{1,0:T(8,128)(2,1)}), bf16[1024,1536]{1,0:T(8,128)(2,1)}) %all-gather.7.cloned.1.call-update) | async-done | bytes 3145744 | tf_op jit(solution)/shard_map/all_gather | solution.py:128
  145.2 5.1 multiply_reduce_fusion.2
  223.3 5.6 fusion.55
  231.5 5.5 multiply_reduce_fusion.1
  328.4 5.8 fusion.54
  336.7 5.3 multiply_reduce_fusion
  424.4 10.0 %all-gather.13.cloned.1.call-done = bf16[1024,1584]{1,0:T(8,128)(2,1)} async-done(((bf16[128,1584]{1,0:T(8,128)(2,1)}), bf16[1024,1584]{1,0:T(8,128)(2,1)}) %all-gather.13.cloned.1.call-update) | async-done | bytes 3244048 | tf_op jit(solution)/shard_map/all_gather | solution.py:210
  444.9 5.0 fusion.85
  449.9 8.7 %fusion.62 = f32[128,12,64]{0,2,1:T(8,128)} fusion(bf16[1024,12,64]{0,2,1:T(8,128)(2,1)} %bitcast.596, f32[12,1024,128]{2,1,0:T(8,128)} %copy-done.22, f32[12,1024]{1,0:T(8,128)} %copy.292, f32[12,1024]{1,0:T(8,128)} %copy.290, bf16[1024,12,64]{0,2,1:T(8,128)(2,1)S(1)} %bitcast.591, bf16[128,12,64]{0,2,1:T(8,128)(2,1)} %bitcast.649), kind=kOutput, calls=%fused_computation.77 | convolution fusion | flops 410517504 | bytes 10125312 | tf_op jit(solution)/shard_map/hqk,qhe->khe/dot_general | solution.py:100
  458.6 6.8 broadcast_multiply_fusion.5
  473.0 7.6 collective-permute-done.2
  519.8 12.5 %all-gather.15.cloned.1.call-done = bf16[1024,1584]{1,0:T(8,128)(2,1)} async-done(((bf16[128,1584]{1,0:T(8,128)(2,1)}), bf16[1024,1584]{1,0:T(8,128)(2,1)}) %all-gather.15.cloned.1.call-update) | async-done | bytes 3244048 | tf_op jit(solution)/shard_map/all_gather | solution.py:210
  550.1 4.6 fusion.88
  554.6 8.8 %fusion.60 = f32[128,12,64]{0,2,1:T(8,128)} fusion(bf16[1024,12,64]{0,2,1:T(8,128)(2,1)} %bitcast.599, f32[12,1024,128]{2,1,0:T(8,128)} %copy-done.23, f32[12,1024]{1,0:T(8,128)} %copy.308, f32[12,1024]{1,0:T(8,128)} %copy.306, bf16[1024,12,64]{0,2,1:T(8,128)(2,1)} %bitcast.592, bf16[128,12,64]{0,2,1:T(8,128)(2,1)} %bitcast.648), kind=kOutput, calls=%fused_computation.75 | convolution fusion | flops 410517504 | bytes 10125312 | tf_op jit(solution)/shard_map/hqk,qhe->khe/dot_general | solution.py:100
  563.5 7.2 broadcast_multiply_fusion.3
  580.2 7.2 collective-permute-done.3
  596.3 5.3 fusion.204
  618.6 5.1 fusion.306
  652.7 4.7 fusion.91
  657.5 8.9 %fusion.58 = f32[128,12,64]{0,2,1:T(8,128)} fusion(bf16[1024,12,64]{0,2,1:T(8,128)(2,1)} %bitcast.595, f32[12,1024,128]{2,1,0:T(8,128)} %copy-done.21, f32[12,1024]{1,0:T(8,128)S(1)} %copy.320, f32[12,1024]{1,0:T(8,128)S(1)} %copy.318, bf16[1024,12,64]{0,2,1:T(8,128)(2,1)} %bitcast.588, bf16[128,12,64]{0,2,1:T(8,128)(2,1)S(1)} %bitcast.647), kind=kOutput, calls=%fused_computation.73 | convolution fusion | flops 410517504 | bytes 10125312 | tf_op jit(solution)/shard_map/hqk,qhe->khe/dot_general | solution.py:100
  666.4 7.6 broadcast_multiply_fusion.1
  689.9 6.6 add_convert_fusion
  696.4 69.7 %scatter_sums.1 = (f32[1,16,128]{2,1,0:T(8,128)S(1)}, f32[1,72,768]{2,1,0:T(8,128)S(1)}, f32[1,48,2304]{2,1,0:T(8,128)S(1)}, f32[1,48,768]{2,1,0:T(8,128)S(1)}, f32[1,48,2304]{2,1,0:T(8,128)S(1)}) custom-call(bf16[16,16,128]{2,1,0:T(8,128)(2,1)S(1)} %fusion.407.refs_0_, bf16[16,72,768]{2,1,0:T(8,128)(2,1)S(1)} %bitcast.538, bf16[16,48,2304]{2,1,0:T(8,128)(2,1)} %bitcast.562, ...), custom_call_target="tpu_custom_call" | custom-call | tf_op jit(solution)/shard_map/scatter_sums/pallas_call | solution.py:468
  (773 shorter events, 429.5 us)
Async XLA Ops:
  7.2 131.1 %all-gather.7.cloned.1.call-start = ((), (), s32[]{:S(2)}) async-start(), calls=%async_computation | async-start | bytes 3538944 | tf_op jit(solution)/shard_map/all_gather | solution.py:128
  97.9 125.4 %all-gather.9.cloned.1.call-start = ((), (), s32[]{:S(2)}) async-start(), calls=%async_computation.1 | async-start | bytes 3538944 | tf_op jit(solution)/shard_map/all_gather | solution.py:128
  98.4 46.8 %copy-start.30 = (f32[2,128,768]{1,2,0:T(8,128)}, f32[2,128,768]{1,2,0:T(8,128)S(1)}, u32[]{:S(2)}) copy-start(f32[2,128,768]{1,2,0:T(8,128)S(1)} %constant_dynamic-update-slice_fusion.4) | copy-start | bytes 2359300
  166.3 8.2 %collective-permute-start = (bf16[128,768]{1,0:T(8,128)(2,1)}, bf16[128,768]{1,0:T(8,128)(2,1)S(1)}, u32[]{:S(2)}, u32[]{:S(2)}) collective-permute-start(bf16[128,768]{1,0:T(8,128)(2,1)} %get-tuple-element.257), channel_id=1, source_target_pairs={{0,16},{1,17},{2,18},{3,19},{4,20},{5,21},{6,22},{7,23},{8,24},{9,... | collective-permute-start | bytes 589832 | tf_op jit(solution)/shard_map/ppermute | solution.py:21
  185.1 143.3 %all-gather.11.cloned.1.call-start = ((), (), s32[]{:S(2)}) async-start(), calls=%async_computation.2 | async-start | bytes 3538944 | tf_op jit(solution)/shard_map/all_gather | solution.py:128
  255.2 8.2 %collective-permute-start.1 = (bf16[128,768]{1,0:T(8,128)(2,1)}, bf16[128,768]{1,0:T(8,128)(2,1)}, u32[]{:S(2)}, u32[]{:S(2)}) collective-permute-start(bf16[128,768]{1,0:T(8,128)(2,1)} %get-tuple-element.265), channel_id=1, source_target_pairs={{0,16},{1,17},{2,18},{3,19},{4,20},{5,21},{6,22},{7,23},{8,24},{9,... | collective-permute-start | bytes 589832 | tf_op jit(solution)/shard_map/ppermute | solution.py:21
  280.6 153.7 %all-gather.13.cloned.1.call-start = ((), (), s32[]{:S(2)}) async-start(), calls=%async_computation.3 | async-start | bytes 3833856 | tf_op jit(solution)/shard_map/all_gather | solution.py:210
  362.4 13.1 %copy-start.168 = (f32[128]{0:T(128)}, f32[128]{0:T(128)S(1)}, u32[]{:S(2)}) copy-start(f32[128]{0:T(128)S(1)} %broadcast_multiply_fusion.22) | copy-start | bytes 1540
  362.6 12.9 %copy-start.182 = (f32[128]{0:T(128)}, f32[128]{0:T(128)S(1)}, u32[]{:S(2)}) copy-start(f32[128]{0:T(128)S(1)} %add_rsqrt_fusion.5) | copy-start | bytes 1540
  393.7 138.6 %all-gather.15.cloned.1.call-start = ((), (), s32[]{:S(2)}) async-start(), calls=%async_computation.4 | async-start | bytes 3833856 | tf_op jit(solution)/shard_map/all_gather | solution.py:210
  467.5 13.0 %copy-start.103 = (bf16[2,1,128,768]{3,2,1,0:T(8,128)(2,1)S(1)}, bf16[2,1,128,768]{3,2,1,0:T(8,128)(2,1)}, u32[]{:S(2)}) copy-start(bf16[2,1,128,768]{3,2,1,0:T(8,128)(2,1)} %param.11) | copy-start | bytes 1179652
  467.6 13.1 %copy-start.203 = (bf16[16,72,768]{2,1,0:T(8,128)(2,1)S(1)}, bf16[16,72,768]{2,1,0:T(8,128)(2,1)}, u32[]{:S(2)}) copy-start(bf16[16,72,768]{2,1,0:T(8,128)(2,1)} %get-tuple-element.22) | copy-start | bytes 5308420
  471.7 8.9 %collective-permute-start.2 = (bf16[128,768]{1,0:T(8,128)(2,1)S(1)}, bf16[128,768]{1,0:T(8,128)(2,1)S(1)}, u32[]{:S(2)}, u32[]{:S(2)}) collective-permute-start(bf16[128,768]{1,0:T(8,128)(2,1)S(1)} %get-tuple-element.87), channel_id=1, source_target_pairs={{16,0},{17,1},{18,2},{19,3},{20,4},{21,5},{22,6},{23,7},{24,8},{25... | collective-permute-start | bytes 589832 | tf_op jit(solution)/shard_map/ppermute | solution.py:21
  473.0 12.2 %copy-start.183 = (f32[128]{0:T(128)}, f32[128]{0:T(128)S(1)}, u32[]{:S(2)}) copy-start(f32[128]{0:T(128)S(1)} %add_rsqrt_fusion.3) | copy-start | bytes 1540
  485.4 12.2 %copy-start.42 = (f32[128,768]{1,0:T(8,128)}, f32[128,768]{1,0:T(8,128)S(1)}, u32[]{:S(2)}) copy-start(f32[128,768]{1,0:T(8,128)S(1)} %multiply_add_fusion.3) | copy-start | bytes 1179652
  485.4 11.5 %copy-start.81 = (bf16[2,128,768]{2,1,0:T(8,128)(2,1)S(1)}, bf16[2,128,768]{2,1,0:T(8,128)(2,1)}, u32[]{:S(2)}) copy-start(bf16[2,128,768]{2,1,0:T(8,128)(2,1)} %copy-done.80) | copy-start | bytes 1179652
  485.4 12.2 %copy-start.91 = (bf16[1,128,12,64]{1,3,2,0:T(8,128)(2,1)S(1)}, bf16[1,128,12,64]{1,3,2,0:T(8,128)(2,1)}, u32[]{:S(2)}) copy-start(bf16[1,128,12,64]{1,3,2,0:T(8,128)(2,1)} %get-tuple-element.158) | copy-start | bytes 589828
  487.8 11.9 %copy-start.106 = (f32[1,128,768]{1,2,0:T(8,128)S(1)}, f32[1,128,768]{1,2,0:T(8,128)}, u32[]{:S(2)}) copy-start(f32[1,128,768]{1,2,0:T(8,128)} %get-tuple-element.75) | copy-start | bytes 1179652
  493.8 142.5 %all-gather.17.cloned.1.call-start = ((), (), s32[]{:S(2)}) async-start(), calls=%async_computation.5 | async-start | bytes 3833856 | tf_op jit(solution)/shard_map/all_gather | solution.py:210
  574.3 13.1 %copy-start.105 = (bf16[2,1,128,768]{3,2,1,0:T(8,128)(2,1)S(1)}, bf16[2,1,128,768]{3,2,1,0:T(8,128)(2,1)}, u32[]{:S(2)}) copy-start(bf16[2,1,128,768]{3,2,1,0:T(8,128)(2,1)} %param.11) | copy-start | bytes 1179652
  574.3 13.1 %copy-start.204 = (bf16[16,72,768]{2,1,0:T(8,128)(2,1)S(1)}, bf16[16,72,768]{2,1,0:T(8,128)(2,1)}, u32[]{:S(2)}) copy-start(bf16[16,72,768]{2,1,0:T(8,128)(2,1)} %get-tuple-element.22) | copy-start | bytes 5308420
  578.5 8.9 %collective-permute-start.3 = (bf16[128,768]{1,0:T(8,128)(2,1)S(1)}, bf16[128,768]{1,0:T(8,128)(2,1)S(1)}, u32[]{:S(2)}, u32[]{:S(2)}) collective-permute-start(bf16[128,768]{1,0:T(8,128)(2,1)S(1)} %get-tuple-element.79), channel_id=1, source_target_pairs={{16,0},{17,1},{18,2},{19,3},{20,4},{21,5},{22,6},{23,7},{24,8},{25... | collective-permute-start | bytes 589832 | tf_op jit(solution)/shard_map/ppermute | solution.py:21
  580.2 11.8 %copy-start.191 = (f32[128]{0:T(128)}, f32[128]{0:T(128)S(1)}, u32[]{:S(2)}) copy-start(f32[128]{0:T(128)S(1)} %add_rsqrt_fusion.1) | copy-start | bytes 1540
  592.2 34.4 %copy-start.44 = (f32[128,768]{1,0:T(8,128)}, f32[128,768]{1,0:T(8,128)S(1)}, u32[]{:S(2)}) copy-start(f32[128,768]{1,0:T(8,128)S(1)} %multiply_add_fusion.1) | copy-start | bytes 1179652
  (196 other events, 690.5 us)
Sparse Core Ops, SparseCore 0:
  98.0 40.2 all-gather.6
  185.2 38.0 all-gather.8
  280.7 38.2 all-gather.10
  393.9 40.4 all-gather.12
  493.9 38.3 all-gather.14
  595.9 38.3 all-gather.16

commit v2 on v1

--- a/solution.py
+++ b/solution.py
@@ -521,7 +521,7 @@
     return (gains[:, 0, :gain_width], qkv, out, gains[:, 1, :gain_width], into, down)
 
 
-def body(
+def staged_body(
     tokens,
     block_order,
     cotangent,
@@ -632,6 +632,286 @@
     )
 
 
+def swap_kernel(cycle, in_ref, out_ref, own_sem, send, recv):
+    me = lax.axis_index("ctx")
+    barrier = pltpu.get_barrier_semaphore()
+    peers = [lax.rem(me + d, cycle) for d in range(1, cycle)]
+    for peer in peers:
+        pl.semaphore_signal(barrier, inc=1, device_id={"ctx": peer}, device_id_type=MESH)
+    pl.semaphore_wait(barrier, cycle - 1)
+    copies = [
+        pltpu.make_async_remote_copy(
+            in_ref.at[peer], out_ref.at[me], send.at[index], recv.at[index],
+            device_id={"ctx": peer}, device_id_type=MESH)
+        for index, peer in enumerate(peers)
+    ]
+    for copy in copies:
+        copy.start()
+    own = pltpu.make_async_copy(in_ref.at[me], out_ref.at[me], own_sem)
+    own.start()
+    own.wait()
+    for copy in copies:
+        copy.wait()
+
+
+def swap(pieces, collective):
+    cycle = pieces.shape[0]
+    return pl.pallas_call(
+        lambda *refs: swap_kernel(cycle, *refs),
+        out_shape=jax.ShapeDtypeStruct(pieces.shape, pieces.dtype),
+        in_specs=[pl.BlockSpec(memory_space=pl.ANY)],
+        out_specs=pl.BlockSpec(memory_space=pl.ANY),
+        scratch_shapes=[
+            pltpu.SemaphoreType.DMA,
+            pltpu.SemaphoreType.DMA((cycle - 1,)),
+            pltpu.SemaphoreType.DMA((cycle - 1,)),
+        ],
+        compiler_params=pltpu.CompilerParams(collective_id=collective, has_side_effects=True),
+        name="swap_narrow" if collective == 2 else "swap_wide",
+    )(pieces)
+
+
+def dot_last(left, right):
+    return lax.dot_general(left, right, (((1,), (1,)), ((), ())), preferred_element_type=jnp.float32)
+
+
+def dot_first(left, right):
+    return lax.dot_general(left, right, (((0,), (0,)), ((), ())), preferred_element_type=jnp.float32)
+
+
+def attend_kernel(width, block, rows_ref, out_ref):
+    start = pl.multiple_of(pl.program_id(0) * block, block)
+    for low in range(0, width, HEAD_DIM):
+        query = rows_ref[pl.ds(start, block), low : low + HEAD_DIM]
+        key = rows_ref[:, width + low : width + low + HEAD_DIM]
+        value = rows_ref[:, 2 * width + low : 2 * width + low + HEAD_DIM]
+        scores = dot_last(query, key) * HEAD_DIM ** (-0.5)
+        exponents = jnp.exp(scores - jnp.max(scores, axis=-1, keepdims=True))
+        total = jnp.sum(exponents, axis=-1, keepdims=True)
+        weighted = jnp.dot(exponents.astype(jnp.bfloat16), value, preferred_element_type=jnp.float32)
+        out_ref[:, low : low + HEAD_DIM] = (weighted / total).astype(jnp.bfloat16)
+
+
+def attend_rows(rows):
+    length, width = rows.shape[0], rows.shape[1] // 3
+    block = min(256, length)
+    return pl.pallas_call(
+        lambda *refs: attend_kernel(width, block, *refs),
+        grid=(length // block,),
+        out_shape=jax.ShapeDtypeStruct((length, width), jnp.bfloat16),
+        in_specs=[pl.BlockSpec(rows.shape, lambda i: (0, 0))],
+        out_specs=pl.BlockSpec((block, width), lambda i: (i, 0)),
+        compiler_params=pltpu.CompilerParams(vmem_limit_bytes=48 * 1024 * 1024),
+        name="attend_rows",
+    )(rows)
+
+
+def attend_back_kernel(width, block, steps, rows_ref, grad_ref, out_ref, key_sum, value_sum):
+    step = pl.program_id(0)
+    start = pl.multiple_of(step * block, block)
+
+    @pl.when(step == 0)
+    def _():
+        key_sum[...] = jnp.zeros_like(key_sum)
+        value_sum[...] = jnp.zeros_like(value_sum)
+
+    scale = HEAD_DIM ** (-0.5)
+    for low in range(0, width, HEAD_DIM):
+        high = low + HEAD_DIM
+        query = rows_ref[pl.ds(start, block), low:high]
+        grad = grad_ref[pl.ds(start, block), low:high]
+        key = rows_ref[:, width + low : width + high]
+        value = rows_ref[:, 2 * width + low : 2 * width + high]
+        scores = dot_last(query, key) * scale
+        exponents = jnp.exp(scores - jnp.max(scores, axis=-1, keepdims=True))
+        probs = exponents * (1.0 / jnp.sum(exponents, axis=-1, keepdims=True))
+        upstream = dot_last(grad, value)
+        delta = jnp.sum(probs * upstream, axis=-1, keepdims=True)
+        grad_scores = (probs * (upstream - delta)).astype(jnp.bfloat16)
+        query_grad = jnp.dot(grad_scores, key, preferred_element_type=jnp.float32) * scale
+        out_ref[pl.ds(start, block), low:high] = query_grad.astype(jnp.bfloat16)
+        key_sum[:, low:high] += dot_first(grad_scores, query)
+        value_sum[:, low:high] += dot_first(probs.astype(jnp.bfloat16), grad)
+
+    @pl.when(step == steps - 1)
+    def _():
+        out_ref[:, width : 2 * width] = (key_sum[...] * scale).astype(jnp.bfloat16)
+        out_ref[:, 2 * width :] = value_sum[...].astype(jnp.bfloat16)
+
+
+def attend_back(rows, grads):
+    length, width = grads.shape
+    block = min(256, length)
+    steps = length // block
+    return pl.pallas_call(
+        lambda *refs: attend_back_kernel(width, block, steps, *refs),
+        grid=(steps,),
+        out_shape=jax.ShapeDtypeStruct(rows.shape, jnp.bfloat16),
+        in_specs=[
+            pl.BlockSpec(rows.shape, lambda i: (0, 0)),
+            pl.BlockSpec(grads.shape, lambda i: (0, 0)),
+        ],
+        out_specs=pl.BlockSpec(rows.shape, lambda i: (0, 0)),
+        scratch_shapes=[pltpu.VMEM(grads.shape, jnp.float32), pltpu.VMEM(grads.shape, jnp.float32)],
+        compiler_params=pltpu.CompilerParams(vmem_limit_bytes=48 * 1024 * 1024),
+        name="attend_back",
+    )(rows, grads)
+
+
+def to_units(values, micro, cycle):
+    groups = cycle // micro
+    rows, kinds = values.shape[0] // micro, values.shape[1] // D
+    parts = values.reshape(micro, rows, kinds, groups, D // groups)
+    return parts.transpose(0, 3, 1, 2, 4).reshape(cycle, rows, kinds * D // groups)
+
+
+def from_units(pieces, micro):
+    cycle, rows, width = pieces.shape
+    groups = cycle // micro
+    kinds = width * groups // D
+    parts = pieces.reshape(micro, groups, rows, kinds, D // groups)
+    return parts.transpose(0, 2, 3, 1, 4).reshape(micro * rows, kinds * D)
+
+
+def to_sequence(values, micro, cycle):
+    kinds = values.shape[1] // D
+    received = swap(to_units(values, micro, cycle), 2 if kinds == 1 else 3)
+    return received.reshape(-1, received.shape[2])
+
+
+def from_sequence(rows, micro, cycle):
+    kinds = 2 if rows.shape[1] * cycle // micro == D else 3
+    received = swap(rows.reshape(cycle, -1, rows.shape[1]), kinds)
+    return from_units(received, micro)
+
+
+def halves(values):
+    half_width = HEAD_DIM // 2
+    first = lax.broadcasted_iota(jnp.int32, values.shape, 1) % HEAD_DIM < half_width
+    return (first, jnp.roll(values, -half_width, axis=1), jnp.roll(values, half_width, axis=1))
+
+
+def turn(values):
+    first, ahead, behind = halves(values)
+    return jnp.where(first, -ahead, behind)
+
+
+def turn_back(values):
+    first, ahead, behind = halves(values)
+    return jnp.where(first, ahead, -behind)
+
+
+def fast_forward(layer_in, cosine, sine, params, micro, cycle):
+    gain_one, w_qkv, w_out, gain_two, w_in, w_down = params
+    normed_one, _ = normalize(layer_in)
+    mixed = jnp.dot(
+        (normed_one * gain_one.astype(jnp.float32)).astype(jnp.bfloat16),
+        w_qkv,
+        preferred_element_type=jnp.float32,
+    )
+    rotated = mixed[:, : 2 * D]
+    rotated = rotated * cosine + turn(rotated) * sine
+    mixed = jnp.concatenate([rotated, mixed[:, 2 * D :]], axis=-1).astype(jnp.bfloat16)
+    rows = to_sequence(mixed, micro, cycle)
+    attended = from_sequence(attend_rows(rows), micro, cycle)
+    hidden = layer_in + jnp.dot(attended, w_out, preferred_element_type=jnp.float32)
+    normed_two, _ = normalize(hidden)
+    gate_up = jnp.dot(
+        (normed_two * gain_two.astype(jnp.float32)).astype(jnp.bfloat16),
+        w_in,
+        preferred_element_type=jnp.float32,
+    )
+    product = (jax.nn.gelu(gate_up[:, :FF], approximate=False) * gate_up[:, FF:]).astype(
+        jnp.bfloat16
+    )
+    layer_out = hidden + jnp.dot(product, w_down, preferred_element_type=jnp.float32)
+    return (layer_out, (layer_in, hidden, gate_up, rows, attended))
+
+
+def fast_backward(upstream, cosine, sine, params, saved, micro, cycle):
+    gain_one, w_qkv, w_out, gain_two, w_in, w_down = params
+    layer_in, hidden, gate_up, rows, attended = saved
+    grad_branch = upstream.astype(jnp.bfloat16)
+    up_part = gate_up[:, FF:]
+    activated, gelu_pull = jax.vjp(
+        lambda gate_in: jax.nn.gelu(gate_in, approximate=False), gate_up[:, :FF]
+    )
+    product = (activated * up_part).astype(jnp.bfloat16)
+    grad_down = dot_first(product, grad_branch)
+    grad_product = dot_last(grad_branch, w_down)
+    grad_gate_up = jnp.concatenate(
+        [gelu_pull(grad_product * up_part)[0], grad_product * activated], axis=-1
+    ).astype(jnp.bfloat16)
+    normed_two, inverse_two = normalize(hidden)
+    gain_two_full = gain_two.astype(jnp.float32)
+    grad_in = dot_first((normed_two * gain_two_full).astype(jnp.bfloat16), grad_gate_up)
+    grad_normed_two = dot_last(grad_gate_up, w_in)
+    grad_gain_two = jnp.sum(grad_normed_two * normed_two, axis=0)
+    grad_hidden = upstream + norm_back(grad_normed_two * gain_two_full, normed_two, inverse_two)
+    grad_attn_out = grad_hidden.astype(jnp.bfloat16)
+    grad_out = dot_first(attended, grad_attn_out)
+    grad_attended = dot_last(grad_attn_out, w_out).astype(jnp.bfloat16)
+    grad_rows = attend_back(rows, to_sequence(grad_attended, micro, cycle))
+    grad_raw = from_sequence(grad_rows, micro, cycle)
+    rotated = grad_raw[:, : 2 * D].astype(jnp.float32)
+    rotated = (rotated * cosine + turn_back(rotated * sine)).astype(jnp.bfloat16)
+    grad_mixed = jnp.concatenate([rotated, grad_raw[:, 2 * D :]], axis=-1)
+    normed_one, inverse_one = normalize(layer_in)
+    gain_one_full = gain_one.astype(jnp.float32)
+    grad_qkv = dot_first((normed_one * gain_one_full).astype(jnp.bfloat16), grad_mixed)
+    grad_normed_one = dot_last(grad_mixed, w_qkv)
+    grad_gain_one = jnp.sum(grad_normed_one * normed_one, axis=0)
+    grad_layer_in = grad_hidden + norm_back(
+        grad_normed_one * gain_one_full, normed_one, inverse_one
+    )
+    return (grad_layer_in, (grad_gain_one, grad_qkv, grad_out, grad_gain_two, grad_in, grad_down))
+
+
+def fast_body(tokens, block_order, cotangent, *weights):
+    section_id = lax.axis_index("section")
+    section_count = lax.axis_size("section")
+    cycle = lax.axis_size("ctx")
+    micro, _, tok_rows, _ = tokens.shape
+    params = gather_params(*weights)
+    blocks = block_order[:, 0, lax.axis_index("ctx")]
+    tables = [rotary(blocks[index], tok_rows) for index in range(micro)]
+    cosine, sine = (
+        jnp.tile(jnp.concatenate([table[kind][:, 0] for table in tables], axis=0), (1, 2 * HEADS))
+        for kind in range(2)
+    )
+    own_rows = tokens[:, 0].reshape(micro * tok_rows, D)
+    upstream_rows = cotangent[:, 0].reshape(micro * tok_rows, D)
+    layer_in = own_rows
+    for tick in range(section_count):
+        layer_out, saved = fast_forward(
+            layer_in.astype(jnp.float32), cosine, sine, params, micro, cycle
+        )
+        outgoing = layer_out.astype(jnp.bfloat16)
+        if tick < section_count - 1:
+            layer_in = jnp.where(section_id == 0, own_rows, shifted(outgoing, "section", 1))
+    section_outs = outgoing
+    upstream = upstream_rows
+    for tick in range(section_count):
+        grad_layer_in, summed = fast_backward(
+            upstream.astype(jnp.float32), cosine, sine, params, saved, micro, cycle
+        )
+        outgoing = grad_layer_in.astype(jnp.bfloat16)
+        if tick < section_count - 1:
+            upstream = jnp.where(
+                section_id == section_count - 1, upstream_rows, shifted(outgoing, "section", -1)
+            )
+    input_grads = jnp.where(section_id == 0, grad_layer_in, outgoing.astype(jnp.float32))
+    shape = (1, micro, 1, tok_rows, D)
+    return (section_outs.reshape(shape), input_grads.reshape(shape)) + scatter_grads(summed)
+
+
+def body(tokens, *rest):
+    micro, cycle = tokens.shape[0], lax.axis_size("ctx")
+    if use_kernels() and cycle % micro == 0 and HEADS % (cycle // micro) == 0:
+        return fast_body(tokens, *rest)
+    return staged_body(tokens, *rest)
+
+
 def solution(mesh):
     in_specs = (
         P(None, "wshard", "ctx", None),

time: 790 us -> 547 us (0.69)
  Pallas kernels: 144 us -> 373 us
  matrix products: 194 us -> 39.4 us
  local copies, waits for them, and re-layouts: 216 us -> 76.3 us
  other arithmetic: 109 us -> 22.6 us
  waiting for transfers between devices: 80.8 us -> 20.6 us
  between operations: 20.9 us -> 3.12 us
    pallas_call x0 -> x12, Pallas kernels: none -> 223 us  [the longest x8 180 us: swap(): pl.pallas_call(lambda *refs: swap_kernel(cycle, *refs), out_shape=jax.Sha...]
    dot_general x57 -> x20, matrix products: 194 us -> 39.4 us  [the longest x8 13.9 us: dot_last(): lax.dot_general(left, right, (((1,), (1,)), ((), ())), preferred_element_...]
    all_gather x6 -> x0, waiting for transfers between devices: 62.9 us -> none  [the longest x3 40.4 us: forward_layer(): lax.all_gather(jnp.concatenate([key_rows, value_rows], axis=-1), 'ctx', a...]
    dynamic_slice x33 -> x0, local copies, waits for them, and re-layouts: 52.4 us -> none  [the longest x23 37.5 us: keep_slot(): previous = lax.dynamic_index_in_dim(buffer, batch_slot, 0, keepdims=False)]
    slice x27 -> x14, local copies, waits for them, and re-layouts: 46 us -> 6.58 us  [the longest x8 5.08 us: halves(): jnp.roll(values, half_width, axis=1)]
    broadcast_in_dim x18 -> x0, local copies, waits for them, and re-layouts: 27.9 us -> none  [the longest x13 25.7 us: keep_slot(): lax.dynamic_update_index_in_dim(buffer, jnp.where(is_valid, value, previo...]
    broadcast_in_dim x11 -> x0, other arithmetic: 24.1 us -> none  [the longest x10 23.2 us: keep_slot(): lax.dynamic_update_index_in_dim(buffer, jnp.where(is_valid, value, previo...]
    reshape x3 -> x10, local copies, waits for them, and re-layouts: 4.35 us -> 22.5 us  [the longest x4 14 us: from_units(): return parts.transpose(0, 2, 3, 1, 4).reshape(micro * rows, kinds * D)]
  transfers between devices with their start and end apart: 10 -> 2, of which waited for: 8 -> 2; matrix products, arithmetic and copies ran while one was open for 23% -> 0% of each run, Pallas kernels for 0% -> 0%
where the time goes in v2:
time: 547 us; the launch traced here: 541 us
  Pallas kernels  373 us (68%)
  local copies, waits for them, and re-layouts  76.3 us (14%)
  matrix products  39.4 us (7%)
  other arithmetic  22.6 us (4%)
  waiting for transfers between devices  20.6 us (4%)
    pallas_call x8, Pallas kernels, swap(): pl.pallas_call(lambda *refs: swap_kernel(cycle, *refs), out_shape=jax.Sha...  180 us
    pallas_call x1, Pallas kernels, scatter_sums(): pl.pallas_call(lambda *refs: scatter_kernel(chips, count, *refs), out_sha...  76 us
    pallas_call x1, Pallas kernels, gather_shards(): pl.pallas_call(lambda *refs: gather_kernel(chips, count, *refs), out_shap...  74.6 us
    pallas_call x2, Pallas kernels, attend_back(): pl.pallas_call(lambda *refs: attend_back_kernel(width, block, steps, *ref...  29 us
    unnamed x119, local copies, waits for them, and re-layouts  23 us
    ppermute x2, waiting for transfers between devices, shifted(): return lax.ppermute(x, axis, pairs)  20.6 us
    pallas_call x2, Pallas kernels, attend_rows(): pl.pallas_call(lambda *refs: attend_kernel(width, block, *refs), grid=(le...  14.2 us
    reshape x4, local copies, waits for them, and re-layouts, from_units(): return parts.transpose(0, 2, 3, 1, 4).reshape(micro * rows, kinds * D)  14 us
  transfers between devices with their start and end apart: 2, of which 2 were waited for; matrix products, arithmetic and copies ran while one was open for 0% of the time, Pallas kernels for 0%

profile of v2, /device:TPU:0, one launch (start us, length us, event | category | flops | bytes accessed | tf_op | source)
XLA Modules:
  0.0 540.8 jit_solution(2069491684291809345)
XLA Ops:
  2.0 74.6 %gather_shards.1 = (bf16[16,16,128]{2,1,0:T(8,128)(2,1)}, bf16[16,48,2304]{2,1,0:T(8,128)(2,1)}, bf16[16,48,768]{2,1,0:T(8,128)(2,1)}, bf16[16,48,2304]{2,1,0:T(8,128)(2,1)}, bf16[16,72,768]{2,1,0:T(8,128)(2,1)}) custom-call(bf16[1,16,128]{2,1,0:T(8,128)(2,1)} %fusion.124.refs_0_, bf16[1,48,2304]{2,1,0:T(8,128)(2,1)} %refs_1_.1, ...), custom_call_target="tpu_custom_call" | custom-call | tf_op jit(solution)/shard_map/gather_shards/pallas_call | solution.py:371
  95.0 3.8 fusion.7
  102.8 3.6 convert_element_type.165
  111.4 26.7 %swap_wide.4 = bf16[8,128,576]{2,1,0:T(8,128)(2,1)} custom-call(bf16[8,128,576]{2,1,0:T(8,128)(2,1)} %copy.30.refs_0_), custom_call_target="tpu_custom_call" | custom-call | tf_op jit(solution)/shard_map/swap_wide/pallas_call | solution.py:659
  139.4 7.1 %attend_rows.2 = bf16[1024,192]{1,0:T(8,128)(2,1)S(1)} custom-call(bf16[1024,576]{1,0:T(8,128)(2,1)S(1)} %bitcast.119), custom_call_target="tpu_custom_call" | custom-call | tf_op jit(solution)/shard_map/attend_rows/pallas_call | solution.py:698
  147.2 19.3 %swap_narrow.4 = bf16[8,128,192]{2,1,0:T(8,128)(2,1)} custom-call(bf16[8,128,192]{2,1,0:T(8,128)(2,1)} %bitcast.121), custom_call_target="tpu_custom_call" | custom-call | tf_op jit(solution)/shard_map/swap_narrow/pallas_call | solution.py:659
  172.4 3.5 fusion.97
  179.2 4.2 collective-permute-start
  183.4 8.7 %collective-permute-done = bf16[256,768]{1,0:T(8,128)(2,1)} collective-permute-done((bf16[256,768]{1,0:T(8,128)(2,1)S(1)}, bf16[256,768]{1,0:T(8,128)(2,1)}, u32[]{:S(2)}, u32[]{:S(2)}) %collective-permute-start) | collective-permute-done | bytes 393248 | tf_op jit(solution)/shard_map/ppermute | solution.py:21
  202.8 27.1 %swap_wide.5 = bf16[8,128,576]{2,1,0:T(8,128)(2,1)} custom-call(bf16[8,128,576]{2,1,0:T(8,128)(2,1)} %copy.36.refs_0_), custom_call_target="tpu_custom_call" | custom-call | tf_op jit(solution)/shard_map/swap_wide/pallas_call | solution.py:659
  231.2 7.1 %attend_rows.3 = bf16[1024,192]{1,0:T(8,128)(2,1)S(1)} custom-call(bf16[1024,576]{1,0:T(8,128)(2,1)S(1)} %bitcast.114), custom_call_target="tpu_custom_call" | custom-call | tf_op jit(solution)/shard_map/attend_rows/pallas_call | solution.py:698
  239.1 19.3 %swap_narrow.5 = bf16[8,128,192]{2,1,0:T(8,128)(2,1)} custom-call(bf16[8,128,192]{2,1,0:T(8,128)(2,1)} %bitcast.122), custom_call_target="tpu_custom_call" | custom-call | tf_op jit(solution)/shard_map/swap_narrow/pallas_call | solution.py:659
  271.7 15.0 %swap_narrow.6 = bf16[8,128,192]{2,1,0:T(8,128)(2,1)} custom-call(bf16[8,128,192]{2,1,0:T(8,128)(2,1)} %bitcast.152), custom_call_target="tpu_custom_call" | custom-call | tf_op jit(solution)/shard_map/swap_narrow/pallas_call | solution.py:659
  287.8 14.7 %attend_back.2 = bf16[1024,576]{1,0:T(8,128)(2,1)S(1)} custom-call(bf16[1024,576]{1,0:T(8,128)(2,1)S(1)} %bitcast.115, bf16[1024,192]{1,0:T(8,128)(2,1)S(1)} %bitcast.124), custom_call_target="tpu_custom_call" | custom-call | tf_op jit(solution)/shard_map/attend_back/pallas_call | solution.py:746
  303.6 27.7 %swap_wide.6 = bf16[8,128,576]{2,1,0:T(8,128)(2,1)} custom-call(bf16[8,128,576]{2,1,0:T(8,128)(2,1)} %bitcast.120), custom_call_target="tpu_custom_call" | custom-call | tf_op jit(solution)/shard_map/swap_wide/pallas_call | solution.py:659
  333.7 3.6 copy.60
  337.3 4.0 reshape.308
  351.5 11.9 %collective-permute-done.1 = bf16[256,768]{1,0:T(8,128)(2,1)} collective-permute-done((bf16[256,768]{1,0:T(8,128)(2,1)}, bf16[256,768]{1,0:T(8,128)(2,1)}, u32[]{:S(2)}, u32[]{:S(2)}) %collective-permute-start.1) | collective-permute-done | bytes 393248 | tf_op jit(solution)/shard_map/ppermute | solution.py:21
  364.5 4.0 add_convert_fusion
  374.9 18.1 %swap_narrow.7 = bf16[8,128,192]{2,1,0:T(8,128)(2,1)} custom-call(bf16[8,128,192]{2,1,0:T(8,128)(2,1)} %bitcast.153), custom_call_target="tpu_custom_call" | custom-call | tf_op jit(solution)/shard_map/swap_narrow/pallas_call | solution.py:659
  394.0 14.3 %attend_back.3 = bf16[1024,576]{1,0:T(8,128)(2,1)S(1)} custom-call(bf16[1024,576]{1,0:T(8,128)(2,1)S(1)} %bitcast.116, bf16[1024,192]{1,0:T(8,128)(2,1)S(1)} %bitcast.123), custom_call_target="tpu_custom_call" | custom-call | tf_op jit(solution)/shard_map/attend_back/pallas_call | solution.py:746
  409.4 26.5 %swap_wide.7 = bf16[8,128,576]{2,1,0:T(8,128)(2,1)} custom-call(bf16[8,128,576]{2,1,0:T(8,128)(2,1)} %bitcast.118), custom_call_target="tpu_custom_call" | custom-call | tf_op jit(solution)/shard_map/swap_wide/pallas_call | solution.py:659
  440.1 4.1 reshape.309
  460.1 76.0 %scatter_sums.1 = (f32[1,16,128]{2,1,0:T(8,128)S(1)}, f32[1,72,768]{2,1,0:T(8,128)S(1)}, f32[1,48,2304]{2,1,0:T(8,128)S(1)}, f32[1,48,768]{2,1,0:T(8,128)S(1)}, f32[1,48,2304]{2,1,0:T(8,128)S(1)}) custom-call(bf16[16,16,128]{2,1,0:T(8,128)(2,1)S(1)} %fusion.113.refs_0_, bf16[16,72,768]{2,1,0:T(8,128)(2,1)S(1)} %bitcast.117, bf16[16,48,2304]{2,1,0:T(8,128)(2,1)} %bitcast.125, ...), custom_call_target="tpu_custom_call" | custom-call | tf_op jit(solution)/shard_map/scatter_sums/pallas_call | solution.py:468
  (225 shorter events, 113.1 us)
Async XLA Ops:
  0.6 78.7 %copy-start.24 = (bf16[2,1,128,768]{3,2,1,0:T(8,128)(2,1)S(1)}, bf16[2,1,128,768]{3,2,1,0:T(8,128)(2,1)}, u32[]{:S(2)}) copy-start(bf16[2,1,128,768]{3,2,1,0:T(8,128)(2,1)} %param.9) | copy-start | bytes 1179652
  82.9 3.8 copy-start.14
  85.3 2.2 copy-start.56
  86.7 8.3 %copy-start.49 = (pred[1536]{0:T(1024)(128)(4,1)}, pred[1536]{0:T(1024)(128)(4,1)S(1)}, u32[]{:S(2)}) copy-start(pred[1536]{0:T(1024)(128)(4,1)S(1)} %fusion.120) | copy-start | bytes 4612
  90.9 107.4 %copy-start.9 = (f32[256,1536]{1,0:T(8,128)}, f32[256,1536]{1,0:T(8,128)S(1)}, u32[]{:S(2)}) copy-start(f32[256,1536]{1,0:T(8,128)S(1)} %copy.26) | copy-start | bytes 4718596
  95.0 103.3 %copy-start.12 = (f32[256,1536]{1,0:T(8,128)}, f32[256,1536]{1,0:T(8,128)S(1)}, u32[]{:S(2)}) copy-start(f32[256,1536]{1,0:T(8,128)S(1)} %copy.27) | copy-start | bytes 4718596
  95.0 3.9 copy-start.38
  172.4 3.5 copy-start.30
  172.4 3.6 copy-start.33
  179.2 12.9 %collective-permute-start = (bf16[256,768]{1,0:T(8,128)(2,1)S(1)}, bf16[256,768]{1,0:T(8,128)(2,1)}, u32[]{:S(2)}, u32[]{:S(2)}) collective-permute-start(bf16[256,768]{1,0:T(8,128)(2,1)S(1)} %fusion.12), channel_id=1, source_target_pairs={{0,16},{1,17},{2,18},{3,19},{4,20},{5,21},{6,22},{7,23},{8,24},{9,... | collective-permute-start | bytes 1179656 | tf_op jit(solution)/shard_map/ppermute | solution.py:21
  239.1 20.6 %copy-start.15 = (bf16[16,48,768]{2,1,0:T(8,128)(2,1)S(1)}, bf16[16,48,768]{2,1,0:T(8,128)(2,1)}, u32[]{:S(2)}) copy-start(bf16[16,48,768]{2,1,0:T(8,128)(2,1)} %get-tuple-element.20) | copy-start | bytes 3538948
  262.8 3.5 copy-start.31
  270.6 16.1 %copy-start.1 = (bf16[8,128,576]{2,1,0:T(8,128)(2,1)S(1)}, bf16[8,128,576]{2,1,0:T(8,128)(2,1)}, u32[]{:S(2)}) copy-start(bf16[8,128,576]{2,1,0:T(8,128)(2,1)} %swap_wide.5) | copy-start | bytes 3538948
  345.0 2.1 slice-start
  348.4 15.0 %copy-start.40 = (bf16[2,1,128,768]{3,2,1,0:T(8,128)(2,1)S(1)}, bf16[2,1,128,768]{3,2,1,0:T(8,128)(2,1)}, u32[]{:S(2)}) copy-start(bf16[2,1,128,768]{3,2,1,0:T(8,128)(2,1)} %param.11) | copy-start | bytes 1179652
  349.4 14.0 %collective-permute-start.1 = (bf16[256,768]{1,0:T(8,128)(2,1)}, bf16[256,768]{1,0:T(8,128)(2,1)}, u32[]{:S(2)}, u32[]{:S(2)}) collective-permute-start(bf16[256,768]{1,0:T(8,128)(2,1)} %fusion.54), channel_id=1, source_target_pairs={{16,0},{17,1},{18,2},{19,3},{20,4},{21,5},{22,6},{23,7},{24,8},{25... | collective-permute-start | bytes 1179656 | tf_op jit(solution)/shard_map/ppermute | solution.py:21
  350.7 13.7 %copy-start.35 = (bf16[16,72,768]{2,1,0:T(8,128)(2,1)S(1)}, bf16[16,72,768]{2,1,0:T(8,128)(2,1)}, u32[]{:S(2)}) copy-start(bf16[16,72,768]{2,1,0:T(8,128)(2,1)} %get-tuple-element.22) | copy-start | bytes 5308420
  364.5 4.0 copy-start.20
  440.0 4.1 copy-start.13
  447.4 3.0 copy-start.11
  451.2 3.1 copy-start.18
  454.3 2.1 copy-start.32
  460.0 76.5 %copy-start.23 = (f32[256,768]{1,0:T(8,128)S(1)}, f32[256,768]{1,0:T(8,128)}, u32[]{:S(2)}) copy-start(f32[256,768]{1,0:T(8,128)} %copy-done.21) | copy-start | bytes 2359300
  460.1 76.5 %copy-start.42 = (f32[256,768]{1,0:T(8,128)S(1)}, f32[256,768]{1,0:T(8,128)}, u32[]{:S(2)}) copy-start(f32[256,768]{1,0:T(8,128)} %get-tuple-element.97) | copy-start | bytes 2359300
  (36 other events, 44.7 us)

commit v3 on v2

--- a/solution.py
+++ b/solution.py
@@ -496,9 +496,9 @@
     gain_width = attn_gain.shape[1]
     gains = jnp.concatenate([attn_gain, mlp_gain], axis=0)
     gains = jnp.pad(gains, ((0, 14), (0, 128 - gain_width)))[None]
-    gains, qkv, out, into, down = gather_shards(
-        (gains, qkv_weight, out_weight, in_weight, down_weight), chips
-    )
+    into = lax.all_gather(in_weight, ("ctx", "wshard"), axis=1, tiled=True)
+    down = lax.all_gather(down_weight, ("ctx", "wshard"), axis=1, tiled=True)
+    gains, qkv, out = gather_shards((gains, qkv_weight, out_weight), chips)
     return (
         gains[:, 0, :gain_width].reshape(D),
         qkv.reshape(D, -1),

time: 547 us -> 553 us (1.011)
  between operations: 3.12 us -> 16.6 us
  other arithmetic: 22.6 us -> 15.4 us
  matrix products: 39.4 us -> 45.1 us
    pallas_call x1, Pallas kernels: 74.6 us -> 56.2 us  [gather_shards(): pl.pallas_call(lambda *refs: gather_kernel(chips, count, *refs), out_shap...]
    pallas_call x8, Pallas kernels: 180 us -> 193 us  [swap(): pl.pallas_call(lambda *refs: swap_kernel(cycle, *refs), out_shape=jax.Sha...]
    unnamed x119 -> x141, local copies, waits for them, and re-layouts: 23 us -> 24.5 us
  transfers between devices with their start and end apart: 2 -> 4, of which waited for: 2 -> 2; matrix products, arithmetic and copies ran while one was open for 0% -> 7% of each run, Pallas kernels for 0% -> 22%
where the time goes in v3:
time: 553 us; the launch traced here: 547 us
  Pallas kernels  369 us (67%)
  local copies, waits for them, and re-layouts  74.5 us (13%)
  matrix products  45.1 us (8%)
  waiting for transfers between devices  21.7 us (4%)
  between operations  16.6 us (3%)
  other arithmetic  15.4 us (3%)
    pallas_call x8, Pallas kernels, swap(): pl.pallas_call(lambda *refs: swap_kernel(cycle, *refs), out_shape=jax.Sha...  193 us
    pallas_call x1, Pallas kernels, scatter_sums(): pl.pallas_call(lambda *refs: scatter_kernel(chips, count, *refs), out_sha...  76.7 us
    pallas_call x1, Pallas kernels, gather_shards(): pl.pallas_call(lambda *refs: gather_kernel(chips, count, *refs), out_shap...  56.2 us
    pallas_call x2, Pallas kernels, attend_back(): pl.pallas_call(lambda *refs: attend_back_kernel(width, block, steps, *ref...  29 us
    unnamed x141, local copies, waits for them, and re-layouts  24.5 us
    ppermute x2, waiting for transfers between devices, shifted(): return lax.ppermute(x, axis, pairs)  20.3 us
    dot_general x8, matrix products, dot_last(): lax.dot_general(left, right, (((1,), (1,)), ((), ())), preferred_element_...  15.2 us
    pallas_call x2, Pallas kernels, attend_rows(): pl.pallas_call(lambda *refs: attend_kernel(width, block, *refs), grid=(le...  14.2 us
  transfers between devices with their start and end apart: 4, of which 2 were waited for; matrix products, arithmetic and copies ran while one was open for 7% of the time, Pallas kernels for 22%

profile of v3, /device:TPU:0, one launch (start us, length us, event | category | flops | bytes accessed | tf_op | source)
XLA Modules:
  0.0 547.5 jit_solution(14357358345597549310)
XLA Ops:
  16.3 56.2 %gather_shards.1 = (bf16[16,16,128]{2,1,0:T(8,128)(2,1)}, bf16[16,48,2304]{2,1,0:T(8,128)(2,1)}, bf16[16,48,768]{2,1,0:T(8,128)(2,1)}) custom-call(bf16[1,16,128]{2,1,0:T(8,128)(2,1)} %fusion.150.refs_0_, bf16[1,48,2304]{2,1,0:T(8,128)(2,1)} %refs_1_.1, bf16[1,48,768]{2,1,0:T(8,128)(2,1)} %refs_2_.1), custom_call_target="tpu_custom_call" | custom-call | tf_op jit(solution)/shard_map/gather_shards/pallas_call | solution.py:371
  83.5 3.5 convert_element_type.165
  92.0 39.4 %swap_wide.4 = bf16[8,128,576]{2,1,0:T(8,128)(2,1)} custom-call(bf16[8,128,576]{2,1,0:T(8,128)(2,1)} %copy.29.refs_0_), custom_call_target="tpu_custom_call" | custom-call | tf_op jit(solution)/shard_map/swap_wide/pallas_call | solution.py:659
  132.8 7.1 %attend_rows.2 = bf16[1024,192]{1,0:T(8,128)(2,1)S(1)} custom-call(bf16[1024,576]{1,0:T(8,128)(2,1)S(1)} %bitcast.143), custom_call_target="tpu_custom_call" | custom-call | tf_op jit(solution)/shard_map/attend_rows/pallas_call | solution.py:698
  140.7 19.3 %swap_narrow.4 = bf16[8,128,192]{2,1,0:T(8,128)(2,1)} custom-call(bf16[8,128,192]{2,1,0:T(8,128)(2,1)} %bitcast.145), custom_call_target="tpu_custom_call" | custom-call | tf_op jit(solution)/shard_map/swap_narrow/pallas_call | solution.py:659
  166.4 4.9 fusion.6
  171.3 6.2 %fusion.40 = bf16[256,768]{1,0:T(8,128)(2,1)} fusion(f32[256,768]{1,0:T(8,128)} %copy-done.32, bf16[1,1152,768]{2,1,0:T(8,128)(2,1)} %all-gather.5.cloned.1.call-done, f32[256,2304]{1,0:T(8,128)} %fusion.6), kind=kOutput, calls=%fused_computation.54 | convolution fusion | flops 472842240 | bytes 5308416 | tf_op jit(solution)/shard_map/dot_general | solution.py:827
  177.5 4.1 collective-permute-start
  181.6 8.8 %collective-permute-done = bf16[256,768]{1,0:T(8,128)(2,1)} collective-permute-done((bf16[256,768]{1,0:T(8,128)(2,1)}, bf16[256,768]{1,0:T(8,128)(2,1)}, u32[]{:S(2)}, u32[]{:S(2)}) %collective-permute-start) | collective-permute-done | bytes 393248 | tf_op jit(solution)/shard_map/ppermute | solution.py:21
  199.7 27.4 %swap_wide.5 = bf16[8,128,576]{2,1,0:T(8,128)(2,1)} custom-call(bf16[8,128,576]{2,1,0:T(8,128)(2,1)} %copy.35.refs_0_), custom_call_target="tpu_custom_call" | custom-call | tf_op jit(solution)/shard_map/swap_wide/pallas_call | solution.py:659
  228.4 7.1 %attend_rows.3 = bf16[1024,192]{1,0:T(8,128)(2,1)S(1)} custom-call(bf16[1024,576]{1,0:T(8,128)(2,1)S(1)} %bitcast.138), custom_call_target="tpu_custom_call" | custom-call | tf_op jit(solution)/shard_map/attend_rows/pallas_call | solution.py:698
  236.3 19.3 %swap_narrow.5 = bf16[8,128,192]{2,1,0:T(8,128)(2,1)} custom-call(bf16[8,128,192]{2,1,0:T(8,128)(2,1)} %bitcast.146), custom_call_target="tpu_custom_call" | custom-call | tf_op jit(solution)/shard_map/swap_narrow/pallas_call | solution.py:659
  271.1 15.0 %swap_narrow.6 = bf16[8,128,192]{2,1,0:T(8,128)(2,1)} custom-call(bf16[8,128,192]{2,1,0:T(8,128)(2,1)} %bitcast.172), custom_call_target="tpu_custom_call" | custom-call | tf_op jit(solution)/shard_map/swap_narrow/pallas_call | solution.py:659
  287.2 14.7 %attend_back.2 = bf16[1024,576]{1,0:T(8,128)(2,1)S(1)} custom-call(bf16[1024,576]{1,0:T(8,128)(2,1)S(1)} %bitcast.139, bf16[1024,192]{1,0:T(8,128)(2,1)S(1)} %bitcast.148), custom_call_target="tpu_custom_call" | custom-call | tf_op jit(solution)/shard_map/attend_back/pallas_call | solution.py:746
  303.0 27.6 %swap_wide.6 = bf16[8,128,576]{2,1,0:T(8,128)(2,1)} custom-call(bf16[8,128,576]{2,1,0:T(8,128)(2,1)} %bitcast.144), custom_call_target="tpu_custom_call" | custom-call | tf_op jit(solution)/shard_map/swap_wide/pallas_call | solution.py:659
  333.1 3.6 copy.57
  336.7 4.0 reshape.308
  352.1 11.5 %collective-permute-done.1 = bf16[256,768]{1,0:T(8,128)(2,1)} collective-permute-done((bf16[256,768]{1,0:T(8,128)(2,1)}, bf16[256,768]{1,0:T(8,128)(2,1)}, u32[]{:S(2)}, u32[]{:S(2)}) %collective-permute-start.1) | collective-permute-done | bytes 393248 | tf_op jit(solution)/shard_map/ppermute | solution.py:21
  364.8 4.1 add_convert_fusion
  375.7 18.1 %swap_narrow.7 = bf16[8,128,192]{2,1,0:T(8,128)(2,1)} custom-call(bf16[8,128,192]{2,1,0:T(8,128)(2,1)} %bitcast.173), custom_call_target="tpu_custom_call" | custom-call | tf_op jit(solution)/shard_map/swap_narrow/pallas_call | solution.py:659
  394.8 14.3 %attend_back.3 = bf16[1024,576]{1,0:T(8,128)(2,1)S(1)} custom-call(bf16[1024,576]{1,0:T(8,128)(2,1)S(1)} %bitcast.140, bf16[1024,192]{1,0:T(8,128)(2,1)S(1)} %bitcast.147), custom_call_target="tpu_custom_call" | custom-call | tf_op jit(solution)/shard_map/attend_back/pallas_call | solution.py:746
  410.2 26.5 %swap_wide.7 = bf16[8,128,576]{2,1,0:T(8,128)(2,1)} custom-call(bf16[8,128,576]{2,1,0:T(8,128)(2,1)} %bitcast.142), custom_call_target="tpu_custom_call" | custom-call | tf_op jit(solution)/shard_map/swap_wide/pallas_call | solution.py:659
  440.7 3.2 reshape.309
  457.4 76.7 %scatter_sums.1 = (f32[1,16,128]{2,1,0:T(8,128)S(1)}, f32[1,72,768]{2,1,0:T(8,128)S(1)}, f32[1,48,2304]{2,1,0:T(8,128)S(1)}, f32[1,48,768]{2,1,0:T(8,128)S(1)}, f32[1,48,2304]{2,1,0:T(8,128)S(1)}) custom-call(bf16[16,16,128]{2,1,0:T(8,128)(2,1)S(1)} %fusion.139.refs_0_, bf16[16,72,768]{2,1,0:T(8,128)(2,1)S(1)} %bitcast.141, bf16[16,48,2304]{2,1,0:T(8,128)(2,1)} %bitcast.149, ...), custom_call_target="tpu_custom_call" | custom-call | tf_op jit(solution)/shard_map/scatter_sums/pallas_call | solution.py:468
  (253 shorter events, 108.2 us)
Async XLA Ops:
  7.2 159.3 %all-gather.3.cloned.1.call-start = ((), (), s32[]{:S(2)}) async-start(), calls=%async_computation | async-start | bytes 3760128 | tf_op jit(solution)/shard_map/all_gather | solution.py:499
  7.9 163.4 %all-gather.5.cloned.1.call-start = ((), (), s32[]{:S(2)}) async-start(), calls=%async_computation.1 | async-start | bytes 1880064 | tf_op jit(solution)/shard_map/all_gather | solution.py:500
  12.1 183.2 %copy-start.11 = (f32[256,1536]{1,0:T(8,128)}, f32[256,1536]{1,0:T(8,128)S(1)}, u32[]{:S(2)}) copy-start(f32[256,1536]{1,0:T(8,128)S(1)} %copy.25) | copy-start | bytes 4718596
  13.7 60.4 %copy-start.28 = (bf16[2,1,128,768]{3,2,1,0:T(8,128)(2,1)S(1)}, bf16[2,1,128,768]{3,2,1,0:T(8,128)(2,1)}, u32[]{:S(2)}) copy-start(bf16[2,1,128,768]{3,2,1,0:T(8,128)(2,1)} %param.9) | copy-start | bytes 1179652
  15.6 179.7 %copy-start.14 = (f32[256,1536]{1,0:T(8,128)}, f32[256,1536]{1,0:T(8,128)S(1)}, u32[]{:S(2)}) copy-start(f32[256,1536]{1,0:T(8,128)S(1)} %copy.26) | copy-start | bytes 4718596
  177.5 12.9 %collective-permute-start = (bf16[256,768]{1,0:T(8,128)(2,1)}, bf16[256,768]{1,0:T(8,128)(2,1)}, u32[]{:S(2)}, u32[]{:S(2)}) collective-permute-start(bf16[256,768]{1,0:T(8,128)(2,1)} %fusion.40), channel_id=1, source_target_pairs={{0,16},{1,17},{2,18},{3,19},{4,20},{5,21},{6,22},{7,23},{8,24},{9,... | collective-permute-start | bytes 1179656 | tf_op jit(solution)/shard_map/ppermute | solution.py:21
  190.7 157.1 %copy-start.60 = (f32[256]{0:T(256)}, f32[256]{0:T(256)S(1)}, u32[]{:S(2)}) copy-start(f32[256]{0:T(256)S(1)} %broadcast_multiply_fusion.9) | copy-start | bytes 3076
  191.4 156.4 %copy-start.62 = (f32[256]{0:T(256)}, f32[256]{0:T(256)S(1)}, u32[]{:S(2)}) copy-start(f32[256]{0:T(256)S(1)} %add_rsqrt_fusion.1) | copy-start | bytes 3076
  236.3 20.6 %copy-start.16 = (bf16[16,48,768]{2,1,0:T(8,128)(2,1)S(1)}, bf16[16,48,768]{2,1,0:T(8,128)(2,1)}, u32[]{:S(2)}) copy-start(bf16[16,48,768]{2,1,0:T(8,128)(2,1)} %get-tuple-element.18) | copy-start | bytes 3538948
  236.3 20.6 %copy-start.18 = (bf16[256,768]{1,0:T(8,128)(2,1)S(1)}, bf16[256,768]{1,0:T(8,128)(2,1)}, u32[]{:S(2)}) copy-start(bf16[256,768]{1,0:T(8,128)(2,1)} %copy-done.17) | copy-start | bytes 1179652
  257.6 187.3 %copy-start.9 = (f32[256,768]{1,0:T(8,128)}, f32[256,768]{1,0:T(8,128)S(1)}, u32[]{:S(2)}) copy-start(f32[256,768]{1,0:T(8,128)S(1)} %get-tuple-element.88) | copy-start | bytes 2359300
  257.7 113.0 %copy-start.56 = (f32[256]{0:T(256)}, f32[256]{0:T(256)S(1)}, u32[]{:S(2)}) copy-start(f32[256]{0:T(256)S(1)} %broadcast_multiply_fusion.8) | copy-start | bytes 3076
  259.3 111.3 %copy-start.58 = (f32[256]{0:T(256)}, f32[256]{0:T(256)S(1)}, u32[]{:S(2)}) copy-start(f32[256]{0:T(256)S(1)} %add_rsqrt_fusion) | copy-start | bytes 3076
  260.5 3.5 copy-start.33
  269.0 17.1 %copy-start.1 = (bf16[8,128,576]{2,1,0:T(8,128)(2,1)S(1)}, bf16[8,128,576]{2,1,0:T(8,128)(2,1)}, u32[]{:S(2)}) copy-start(bf16[8,128,576]{2,1,0:T(8,128)(2,1)} %swap_wide.5) | copy-start | bytes 3538948
  348.9 14.7 %collective-permute-start.1 = (bf16[256,768]{1,0:T(8,128)(2,1)}, bf16[256,768]{1,0:T(8,128)(2,1)}, u32[]{:S(2)}, u32[]{:S(2)}) collective-permute-start(bf16[256,768]{1,0:T(8,128)(2,1)} %fusion.83), channel_id=1, source_target_pairs={{16,0},{17,1},{18,2},{19,3},{20,4},{21,5},{22,6},{23,7},{24,8},{25... | collective-permute-start | bytes 1179656 | tf_op jit(solution)/shard_map/ppermute | solution.py:21
  350.2 14.6 %copy-start.40 = (bf16[1,1152,768]{2,1,0:T(8,128)(2,1)S(1)}, bf16[1,1152,768]{2,1,0:T(8,128)(2,1)}, u32[]{:S(2)}) copy-start(bf16[1,1152,768]{2,1,0:T(8,128)(2,1)} %all-gather.5.cloned.1.call-done) | copy-start | bytes 5308420
  364.8 5.9 %copy-start.35 = (bf16[256,768]{1,0:T(8,128)(2,1)}, bf16[256,768]{1,0:T(8,128)(2,1)S(1)}, u32[]{:S(2)}) copy-start(bf16[256,768]{1,0:T(8,128)(2,1)S(1)} %broadcast_select_fusion) | copy-start | bytes 1179652
  364.8 4.1 copy-start.24
  440.7 3.3 copy-start.15
  450.1 3.1 copy-start.22
  457.4 77.3 %copy-start.27 = (f32[256,768]{1,0:T(8,128)S(1)}, f32[256,768]{1,0:T(8,128)}, u32[]{:S(2)}) copy-start(f32[256,768]{1,0:T(8,128)} %copy-done.25) | copy-start | bytes 2359300
  457.4 77.3 %copy-start.45 = (f32[256,768]{1,0:T(8,128)S(1)}, f32[256,768]{1,0:T(8,128)}, u32[]{:S(2)}) copy-start(f32[256,768]{1,0:T(8,128)} %get-tuple-element.93) | copy-start | bytes 2359300
  457.4 78.5 %copy-start.41 = (bf16[1,1152,768]{2,1,0:T(8,128)(2,1)S(1)}, bf16[1,1152,768]{2,1,0:T(8,128)(2,1)}, u32[]{:S(2)}) copy-start(bf16[1,1152,768]{2,1,0:T(8,128)(2,1)} %all-gather.5.cloned.1.call-done) | copy-start | bytes 5308420
  (49 other events, 66.5 us)
Sparse Core Ops, SparseCore 0:
  10.3 68.9 all-gather.2
  81.5 48.6 all-gather.4
